TPU v7x, 128 devices: a whole 4x4x4 slice. The times are simulated.
128 devices in a mesh: member: 8 (over y, core), lon: 16 (over x, z).
Axes of the slice: x: 4, y: 4, z: 4, core: 2. Of those that a mesh axis runs over, the one named last changes fastest.
Arguments:
- ensemble: float32 [96, 3, 64, 4096], P('member', None, None, 'lon')
- perturbation: float32 [96, 3, 64, 4096], P('member', None, None, 'lon'), may hold values from -2.4 to 2.4
- observed: float32 [64, 4096], P(None, 'lon'), may hold values from -6 to 6
- precision: float32 [64, 4096], P(None, 'lon'), may hold values from 0.1 to 1
- nudging: float32 [64, 4096], P(None, 'lon'), may hold values from 0.05 to 0.3
- ancestors: int32 [96], replicated, may hold values from 0 to 95, as said below
Outputs:
- weights: float32 [96], P('member')
- analysis: float32 [96, 3, 64, 4096], P('member', None, None, 'lon')
Inputs may be any that keep to these rules, and one draw needn't show every extreme that they name: Number the particles in blocks of 12 (block b holds particles b * 12 to (b + 1) * 12 - 1). Within each block of new particles, at most 3 have ancestors in any one block of old particles, and in every block of new particles some one block of old particles is named exactly 3 times.
All inputs are finite; a program needn't handle non-finite values.
Results may differ from a plain program's by a relative error of at most 0.0003.
Values sent between devices are 32-bit elements; how exact they have to be, the bound alone decides.
A program may use at most 128 MiB of HBM per device.

v0:
```python
import jax
import jax.numpy as jnp
from jax import lax
from jax.sharding import PartitionSpec as P

STEPS = 3


gravity_term = 0.25
depth_term = 0.25


def with_halo(value, sides, width):
    for axis, dim in sides:
        size, length = (lax.axis_size(axis), value.shape[dim])
        up = [(i, (i + 1) % size) for i in range(size)]
        down = [(j, i) for i, j in up]
        last = lax.slice_in_dim(value, length - width, length, axis=dim)
        first = lax.slice_in_dim(value, 0, width, axis=dim)
        before = lax.ppermute(last, axis, up)
        after = lax.ppermute(first, axis, down)
        value = jnp.concatenate([before, value, after], axis=dim)
    return value


def across(q):
    return (q[..., 2:] - q[..., :-2]) * 0.5


def along(q):
    padded = jnp.pad(q, ((0, 0), (1, 1), (0, 0)))
    return (padded[:, 2:] - padded[:, :-2]) * 0.5


def body(ensemble, perturbation, observed, precision, nudging, ancestors):
    count = ensemble.shape[0]
    lat = ensemble.shape[2]
    clon = ensemble.shape[3]
    rows = jnp.arange(lat).astype(jnp.float32)
    coriolis = (0.3 * jnp.sin(jnp.pi * (rows + 0.5 - lat / 2) / lat))[:, None]
    state = ensemble
    for step in range(STEPS):
        u, v, h = (state[:, 0], state[:, 1], state[:, 2])
        h_wide = with_halo(h, (("lon", 2),), 1)
        u_new = u + coriolis * v - gravity_term * across(h_wide)
        v_new = v - coriolis * u - gravity_term * along(h)
        u_wide = with_halo(u_new, (("lon", 2),), 1)
        h_new = (
            h
            - depth_term * (across(u_wide) + along(v_new))
            + nudging * (observed - h)
            + perturbation[:, step]
        )
        state = jnp.stack([u_new, v_new, h_new], axis=1)
    residual = observed - state[:, 2]
    partial_sum = jnp.sum(precision * residual * residual, axis=(1, 2))
    cells = lat * clon * lax.axis_size("lon")
    offset = lax.axis_index("member") * count
    weight_totals = lax.psum(partial_sum, "lon")
    own_logw = weight_totals * (-2.0 / cells)
    every_logw = lax.all_gather(own_logw, "member", axis=0, tiled=True)
    normalized = jax.nn.softmax(every_logw)
    weights = lax.dynamic_slice_in_dim(normalized, offset, count)
    wanted = lax.dynamic_slice_in_dim(ancestors, offset, count)
    piece = lax.all_gather(state, "member", axis=0, tiled=True)
    pieces = piece.shape[0]
    select = (wanted[:, None] == jnp.arange(pieces, dtype=jnp.int32)[None, :]).astype(jnp.float32)
    analysis = jnp.einsum("jn,nfyx->jfyx", select, piece, precision=lax.Precision.HIGHEST)
    return (weights, analysis)


def solution(mesh):
    placed = (
        P("member", None, None, "lon"),
        P("member", None, None, "lon"),
        P(None, "lon"),
        P(None, "lon"),
        P(None, "lon"),
        P(),
    )
    return jax.shard_map(
        body,
        mesh=mesh,
        in_specs=placed,
        out_specs=(P("member"), P("member", None, None, "lon")),
        check_vma=False,
    )
```

profile of v0, /device:TPU:1, one launch (start us, length us, event | category | flops | bytes accessed | tf_op | source)
XLA Modules:
  0.0 218.6 jit_solution(1171308869463061435)
XLA Ops:
  7.2 0.0 copy-start
  7.2 0.0 all-gather.2.cloned.1.call-start
  7.2 1.3 slice_bitcast_fusion
  8.6 0.2 fusion.53
  8.7 6.8 %collective-permute-start = (f32[12,64,1]{2,1,0:T(8,128)S(1)}, f32[12,64,1]{2,1,0:T(8,128)S(1)}, u32[]{:S(2)}, u32[]{:S(2)}) collective-permute-start(f32[12,64,1]{2,1,0:T(8,128)S(1)} %get-tuple-element.24), channel_id=1, source_target_pairs={{1,0},{2,1},{3,2},{4,3},{5,4},{6,5},{7,6},{8,7},{9,8},{10,9},{11,1... | collective-permute-start | bytes 9224 | tf_op jit(solution)/shard_map/ppermute | solution.py:21
  15.6 0.0 collective-permute-start.1
  15.6 0.0 copy-start.1
  15.6 0.0 copy-start.2
  15.7 0.0 copy-start.3
  15.7 7.7 %collective-permute-done = f32[12,64,1]{2,1,0:T(8,128)S(1)} collective-permute-done((f32[12,64,1]{2,1,0:T(8,128)S(1)}, f32[12,64,1]{2,1,0:T(8,128)S(1)}, u32[]{:S(2)}, u32[]{:S(2)}) %collective-permute-start) | collective-permute-done | bytes 3104 | tf_op jit(solution)/shard_map/ppermute | solution.py:21
  23.4 5.2 %collective-permute-done.1 = f32[12,64,1]{2,1,0:T(8,128)S(1)} collective-permute-done((f32[12,64,1]{2,1,0:T(8,128)S(1)}, f32[12,64,1]{2,1,0:T(8,128)S(1)}, u32[]{:S(2)}, u32[]{:S(2)}) %collective-permute-start.1) | collective-permute-done | bytes 3104 | tf_op jit(solution)/shard_map/ppermute | solution.py:20
  28.6 0.0 copy-done
  28.6 0.7 fusion.41
  29.2 0.2 fusion.52
  29.4 0.4 collective-permute-start.2
  29.8 1.1 collective-permute-start.3
  31.0 7.3 %collective-permute-done.2 = f32[12,64,1]{2,1,0:T(8,128)S(1)} collective-permute-done((f32[12,64,1]{2,1,0:T(8,128)S(1)}, f32[12,64,1]{2,1,0:T(8,128)S(1)}, u32[]{:S(2)}, u32[]{:S(2)}) %collective-permute-start.2) | collective-permute-done | bytes 3104 | tf_op jit(solution)/shard_map/ppermute | solution.py:21
  38.2 3.7 %collective-permute-done.3 = f32[12,64,1]{2,1,0:T(8,128)S(1)} collective-permute-done((f32[12,64,1]{2,1,0:T(8,128)S(1)}, f32[12,64,1]{2,1,0:T(8,128)S(1)}, u32[]{:S(2)}, u32[]{:S(2)}) %collective-permute-start.3) | collective-permute-done | bytes 3104 | tf_op jit(solution)/shard_map/ppermute | solution.py:20
  41.9 0.0 copy-done.1
  41.9 0.0 copy-done.2
  41.9 0.0 copy-done.3
  41.9 0.7 fusion.10
  42.6 0.2 fusion.51
  42.8 0.4 collective-permute-start.4
  43.1 1.2 collective-permute-start.5
  44.3 6.4 %collective-permute-done.4 = f32[12,64,1]{2,1,0:T(8,128)S(1)} collective-permute-done((f32[12,64,1]{2,1,0:T(8,128)S(1)}, f32[12,64,1]{2,1,0:T(8,128)S(1)}, u32[]{:S(2)}, u32[]{:S(2)}) %collective-permute-start.4) | collective-permute-done | bytes 3104 | tf_op jit(solution)/shard_map/ppermute | solution.py:21
  50.7 3.6 %collective-permute-done.5 = f32[12,64,1]{2,1,0:T(8,128)S(1)} collective-permute-done((f32[12,64,1]{2,1,0:T(8,128)S(1)}, f32[12,64,1]{2,1,0:T(8,128)S(1)}, u32[]{:S(2)}, u32[]{:S(2)}) %collective-permute-start.5) | collective-permute-done | bytes 3104 | tf_op jit(solution)/shard_map/ppermute | solution.py:20
  54.3 0.7 fusion.37
  55.0 0.2 fusion.50
  55.2 0.4 collective-permute-start.6
  55.5 1.2 collective-permute-start.7
  56.7 5.5 %collective-permute-done.6 = f32[12,64,1]{2,1,0:T(8,128)S(1)} collective-permute-done((f32[12,64,1]{2,1,0:T(8,128)S(1)}, f32[12,64,1]{2,1,0:T(8,128)S(1)}, u32[]{:S(2)}, u32[]{:S(2)}) %collective-permute-start.6) | collective-permute-done | bytes 3104 | tf_op jit(solution)/shard_map/ppermute | solution.py:21
  62.2 3.6 %collective-permute-done.7 = f32[12,64,1]{2,1,0:T(8,128)S(1)} collective-permute-done((f32[12,64,1]{2,1,0:T(8,128)S(1)}, f32[12,64,1]{2,1,0:T(8,128)S(1)}, u32[]{:S(2)}, u32[]{:S(2)}) %collective-permute-start.7) | collective-permute-done | bytes 3104 | tf_op jit(solution)/shard_map/ppermute | solution.py:20
  65.8 0.6 fusion.19
  66.4 0.2 fusion.49
  66.6 0.4 collective-permute-start.8
  67.0 0.0 copy-start.4
  67.0 1.2 collective-permute-start.9
  68.2 5.2 %collective-permute-done.8 = f32[12,64,1]{2,1,0:T(8,128)S(1)} collective-permute-done((f32[12,64,1]{2,1,0:T(8,128)S(1)}, f32[12,64,1]{2,1,0:T(8,128)S(1)}, u32[]{:S(2)}, u32[]{:S(2)}) %collective-permute-start.8) | collective-permute-done | bytes 3104 | tf_op jit(solution)/shard_map/ppermute | solution.py:21
  73.3 3.6 %collective-permute-done.9 = f32[12,64,1]{2,1,0:T(8,128)S(1)} collective-permute-done((f32[12,64,1]{2,1,0:T(8,128)S(1)}, f32[12,64,1]{2,1,0:T(8,128)S(1)}, u32[]{:S(2)}, u32[]{:S(2)}) %collective-permute-start.9) | collective-permute-done | bytes 3104 | tf_op jit(solution)/shard_map/ppermute | solution.py:20
  76.9 0.7 fusion.33
  77.6 0.2 fusion.48
  77.8 0.1 collective-permute-start.10
  77.9 1.5 collective-permute-start.11
  79.3 5.2 %collective-permute-done.10 = f32[12,64,1]{2,1,0:T(8,128)S(1)} collective-permute-done((f32[12,64,1]{2,1,0:T(8,128)S(1)}, f32[12,64,1]{2,1,0:T(8,128)S(1)}, u32[]{:S(2)}, u32[]{:S(2)}) %collective-permute-start.10) | collective-permute-done | bytes 3104 | tf_op jit(solution)/shard_map/ppermute | solution.py:21
  84.5 3.4 %collective-permute-done.11 = f32[12,64,1]{2,1,0:T(8,128)S(1)} collective-permute-done((f32[12,64,1]{2,1,0:T(8,128)S(1)}, f32[12,64,1]{2,1,0:T(8,128)S(1)}, u32[]{:S(2)}, u32[]{:S(2)}) %collective-permute-start.11) | collective-permute-done | bytes 3104 | tf_op jit(solution)/shard_map/ppermute | solution.py:20
  87.9 0.0 copy-done.4
  87.9 0.8 fusion.29
  88.7 1.6 pad_maximum_fusion
  90.2 0.0 all-gather.2.cloned.1.call-update
  90.3 0.6 copy-done.6
  90.9 0.6 dynamic-slice
  92.1 0.0 copy-done.5
  92.1 0.1 dynamic_slice.7
  92.2 28.5 %psum.7 = f32[12]{0:T(128)S(1)} all-reduce(f32[12]{0:T(128)S(1)} %get-tuple-element.6), channel_id=1, replica_groups=mesh['member'=8,'lon'=16] {'lon'}, use_global_device_ids=true, to_apply=%region_1.2 | all-reduce | flops 12 | bytes 96 | tf_op jit(solution)/shard_map/psum | solution.py:59
  120.7 0.1 multiply_dynamic-update-slice_fusion
  120.8 26.5 %all-reduce.6 = f32[96]{0:T(128)S(1)} all-reduce(f32[96]{0:T(128)S(1)} %multiply_dynamic-update-slice_fusion), channel_id=1, replica_groups=mesh['member'=8,'lon'=16] {'member'}, use_global_device_ids=true, to_apply=%add.6 | all-reduce | flops 96 | bytes 768
  147.3 0.6 reduce_max.9
  147.9 1.2 fusion.46
  149.2 1.2 broadcast_divide_fusion
  150.4 0.6 dynamic_slice.6
  151.0 36.5 %all-gather.2.cloned.1.call-done = f32[96,3,64,256]{3,2,1,0:T(8,128)} async-done(((f32[12,3,64,256]{3,2,1,0:T(8,128)}), f32[96,3,64,256]{3,2,1,0:T(8,128)}) %all-gather.2.cloned.1.call-update) | async-done | bytes 18874384 | tf_op jit(solution)/shard_map/all_gather | solution.py:65
  187.5 21.5 %fusion = f32[12,3,64,256]{3,0,2,1:T(8,128)S(1)} fusion(f32[96,3,64,256]{3,2,1,0:T(8,128)} %all-gather.2.cloned.1.call-done, s32[12]{0:T(128)S(1)} %dynamic_slice.7), kind=kOutput, calls=%fused_computation | convolution fusion | flops 679478400 | bytes 21233712 | tf_op jit(solution)/shard_map/jn,nfyx->jfyx/dot_general | solution.py:68
  209.0 2.8 %copy.24 = f32[12,3,64,256]{3,2,1,0:T(8,128)} copy(f32[12,3,64,256]{3,0,2,1:T(8,128)S(1)} %fusion) | data formatting | bytes 4718592
  (4 shorter events, 0.0 us)
Async XLA Ops:
  7.2 21.4 %copy-start = (f32[12,3,64,256]{3,2,1,0:T(8,128)S(1)}, f32[12,3,64,256]{3,2,1,0:T(8,128)}, u32[]{:S(2)}) copy-start(f32[12,3,64,256]{3,2,1,0:T(8,128)} %param.6) | copy-start | bytes 7077892
  7.2 180.3 %all-gather.2.cloned.1.call-start = ((), (), s32[]{:S(2)}) async-start(), calls=%async_computation | async-start | bytes 21233664 | tf_op jit(solution)/shard_map/all_gather | solution.py:65
  8.7 14.6 %collective-permute-start = (f32[12,64,1]{2,1,0:T(8,128)S(1)}, f32[12,64,1]{2,1,0:T(8,128)S(1)}, u32[]{:S(2)}, u32[]{:S(2)}) collective-permute-start(f32[12,64,1]{2,1,0:T(8,128)S(1)} %get-tuple-element.24), channel_id=1, source_target_pairs={{1,0},{2,1},{3,2},{4,3},{5,4},{6,5},{7,6},{8,7},{9,8},{10,9},{11,1... | collective-permute-start | bytes 9224 | tf_op jit(solution)/shard_map/ppermute | solution.py:21
  15.6 13.0 %collective-permute-start.1 = (f32[12,64,1]{2,1,0:T(8,128)S(1)}, f32[12,64,1]{2,1,0:T(8,128)S(1)}, u32[]{:S(2)}, u32[]{:S(2)}) collective-permute-start(f32[12,64,1]{2,1,0:T(8,128)S(1)} %get-tuple-element.25), channel_id=1, source_target_pairs={{0,1},{1,2},{2,3},{3,4},{4,5},{5,6},{6,7},{7,8},{8,9},{9,10},{10,1... | collective-permute-start | bytes 9224 | tf_op jit(solution)/shard_map/ppermute | solution.py:20
  15.6 26.3 %copy-start.1 = (f32[12,3,64,256]{3,2,1,0:T(8,128)S(1)}, f32[12,3,64,256]{3,2,1,0:T(8,128)}, u32[]{:S(2)}) copy-start(f32[12,3,64,256]{3,2,1,0:T(8,128)} %param.7) | copy-start | bytes 7077892
  15.6 26.3 %copy-start.2 = (f32[64,256]{1,0:T(8,128)S(1)}, f32[64,256]{1,0:T(8,128)}, u32[]{:S(2)}) copy-start(f32[64,256]{1,0:T(8,128)} %param.8) | copy-start | bytes 196612
  15.7 26.3 %copy-start.3 = (f32[64,256]{1,0:T(8,128)S(1)}, f32[64,256]{1,0:T(8,128)}, u32[]{:S(2)}) copy-start(f32[64,256]{1,0:T(8,128)} %param.10) | copy-start | bytes 196612
  29.4 8.8 %collective-permute-start.2 = (f32[12,64,1]{2,1,0:T(8,128)S(1)}, f32[12,64,1]{2,1,0:T(8,128)S(1)}, u32[]{:S(2)}, u32[]{:S(2)}) collective-permute-start(f32[12,64,1]{2,1,0:T(8,128)S(1)} %get-tuple-element.22), channel_id=1, source_target_pairs={{1,0},{2,1},{3,2},{4,3},{5,4},{6,5},{7,6},{8,7},{9,8},{10,9},{11,1... | collective-permute-start | bytes 9224 | tf_op jit(solution)/shard_map/ppermute | solution.py:21
  29.8 12.1 %collective-permute-start.3 = (f32[12,64,1]{2,1,0:T(8,128)S(1)}, f32[12,64,1]{2,1,0:T(8,128)S(1)}, u32[]{:S(2)}, u32[]{:S(2)}) collective-permute-start(f32[12,64,1]{2,1,0:T(8,128)S(1)} %get-tuple-element.23), channel_id=1, source_target_pairs={{0,1},{1,2},{2,3},{3,4},{4,5},{5,6},{6,7},{7,8},{8,9},{9,10},{10,1... | collective-permute-start | bytes 9224 | tf_op jit(solution)/shard_map/ppermute | solution.py:20
  42.8 7.9 %collective-permute-start.4 = (f32[12,64,1]{2,1,0:T(8,128)S(1)}, f32[12,64,1]{2,1,0:T(8,128)S(1)}, u32[]{:S(2)}, u32[]{:S(2)}) collective-permute-start(f32[12,64,1]{2,1,0:T(8,128)S(1)} %get-tuple-element.20), channel_id=1, source_target_pairs={{1,0},{2,1},{3,2},{4,3},{5,4},{6,5},{7,6},{8,7},{9,8},{10,9},{11,1... | collective-permute-start | bytes 9224 | tf_op jit(solution)/shard_map/ppermute | solution.py:21
  43.1 11.2 %collective-permute-start.5 = (f32[12,64,1]{2,1,0:T(8,128)S(1)}, f32[12,64,1]{2,1,0:T(8,128)S(1)}, u32[]{:S(2)}, u32[]{:S(2)}) collective-permute-start(f32[12,64,1]{2,1,0:T(8,128)S(1)} %get-tuple-element.21), channel_id=1, source_target_pairs={{0,1},{1,2},{2,3},{3,4},{4,5},{5,6},{6,7},{7,8},{8,9},{9,10},{10,1... | collective-permute-start | bytes 9224 | tf_op jit(solution)/shard_map/ppermute | solution.py:20
  55.2 7.0 %collective-permute-start.6 = (f32[12,64,1]{2,1,0:T(8,128)S(1)}, f32[12,64,1]{2,1,0:T(8,128)S(1)}, u32[]{:S(2)}, u32[]{:S(2)}) collective-permute-start(f32[12,64,1]{2,1,0:T(8,128)S(1)} %get-tuple-element.18), channel_id=1, source_target_pairs={{1,0},{2,1},{3,2},{4,3},{5,4},{6,5},{7,6},{8,7},{9,8},{10,9},{11,1... | collective-permute-start | bytes 9224 | tf_op jit(solution)/shard_map/ppermute | solution.py:21
  55.5 10.3 %collective-permute-start.7 = (f32[12,64,1]{2,1,0:T(8,128)S(1)}, f32[12,64,1]{2,1,0:T(8,128)S(1)}, u32[]{:S(2)}, u32[]{:S(2)}) collective-permute-start(f32[12,64,1]{2,1,0:T(8,128)S(1)} %get-tuple-element.19), channel_id=1, source_target_pairs={{0,1},{1,2},{2,3},{3,4},{4,5},{5,6},{6,7},{7,8},{8,9},{9,10},{10,1... | collective-permute-start | bytes 9224 | tf_op jit(solution)/shard_map/ppermute | solution.py:20
  66.6 6.7 %collective-permute-start.8 = (f32[12,64,1]{2,1,0:T(8,128)S(1)}, f32[12,64,1]{2,1,0:T(8,128)S(1)}, u32[]{:S(2)}, u32[]{:S(2)}) collective-permute-start(f32[12,64,1]{2,1,0:T(8,128)S(1)} %get-tuple-element.16), channel_id=1, source_target_pairs={{1,0},{2,1},{3,2},{4,3},{5,4},{6,5},{7,6},{8,7},{9,8},{10,9},{11,1... | collective-permute-start | bytes 9224 | tf_op jit(solution)/shard_map/ppermute | solution.py:21
  67.0 20.9 %copy-start.4 = (f32[64,256]{1,0:T(8,128)S(1)}, f32[64,256]{1,0:T(8,128)}, u32[]{:S(2)}) copy-start(f32[64,256]{1,0:T(8,128)} %param.9) | copy-start | bytes 196612
  67.0 9.9 %collective-permute-start.9 = (f32[12,64,1]{2,1,0:T(8,128)S(1)}, f32[12,64,1]{2,1,0:T(8,128)S(1)}, u32[]{:S(2)}, u32[]{:S(2)}) collective-permute-start(f32[12,64,1]{2,1,0:T(8,128)S(1)} %get-tuple-element.17), channel_id=1, source_target_pairs={{0,1},{1,2},{2,3},{3,4},{4,5},{5,6},{6,7},{7,8},{8,9},{9,10},{10,1... | collective-permute-start | bytes 9224 | tf_op jit(solution)/shard_map/ppermute | solution.py:20
  77.8 6.7 %collective-permute-start.10 = (f32[12,64,1]{2,1,0:T(8,128)S(1)}, f32[12,64,1]{2,1,0:T(8,128)S(1)}, u32[]{:S(2)}, u32[]{:S(2)}) collective-permute-start(f32[12,64,1]{2,1,0:T(8,128)S(1)} %get-tuple-element.14), channel_id=1, source_target_pairs={{1,0},{2,1},{3,2},{4,3},{5,4},{6,5},{7,6},{8,7},{9,8},{10,9},{11,1... | collective-permute-start | bytes 9224 | tf_op jit(solution)/shard_map/ppermute | solution.py:21
  77.9 10.0 %collective-permute-start.11 = (f32[12,64,1]{2,1,0:T(8,128)S(1)}, f32[12,64,1]{2,1,0:T(8,128)S(1)}, u32[]{:S(2)}, u32[]{:S(2)}) collective-permute-start(f32[12,64,1]{2,1,0:T(8,128)S(1)} %get-tuple-element.15), channel_id=1, source_target_pairs={{0,1},{1,2},{2,3},{3,4},{4,5},{5,6},{6,7},{7,8},{8,9},{9,10},{10,1... | collective-permute-start | bytes 9224 | tf_op jit(solution)/shard_map/ppermute | solution.py:20
  90.2 0.7 copy-start.6
  90.2 1.9 copy-start.5
Sparse Core Ops, SparseCore 0:
  90.4 97.0 all-gather.1
where the time goes:
time: 219 us
  waiting for transfers between devices  96.8 us (44%)
  blocking collectives  55 us (25%)
  matrix products  21.5 us (10%)
  between operations  14.8 us (7%)
  starting transfers between devices  14.6 us (7%)
  other arithmetic  8.9 us (4%)
  local copies, waits for them, and re-layouts  7.03 us (3%)
    ppermute x6, waiting for transfers between devices, with_halo(): after = lax.ppermute(first, axis, down)  37.2 us
    all_gather x1, waiting for transfers between devices, body(): piece = lax.all_gather(state, 'member', axis=0, tiled=True)  36.5 us
    psum x1, blocking collectives, body(): weight_totals = lax.psum(partial_sum, 'lon')  28.5 us
    unnamed x1, blocking collectives  26.5 us
    ppermute x6, waiting for transfers between devices, with_halo(): before = lax.ppermute(last, axis, up)  23.1 us
    dot_general x1, matrix products, body(): jnp.einsum('jn,nfyx->jfyx', select, piece, precision=lax.Precision.HIGHEST)  21.5 us
    ppermute x6, starting transfers between devices, with_halo(): after = lax.ppermute(first, axis, down)  8.38 us
    ppermute x6, starting transfers between devices, with_halo(): before = lax.ppermute(last, axis, up)  6.14 us
  transfers between devices with their start and end apart: 13, of which 13 were waited for; matrix products, arithmetic and copies ran while one was open for 2% of the time, Pallas kernels for 0%

commit v1 on v0

v1 whole, which is shorter than its diff:
```python
import functools
import math

import jax
import jax.numpy as jnp
import numpy as np
from jax import lax
from jax.experimental import pallas as pl
from jax.experimental.pallas import tpu as pltpu
from jax.sharding import PartitionSpec as P

MESH = pl.DeviceIdType.MESH
F32 = jnp.float32
STEPS = 3
LAT = 64
CLON = 256
PART = 12
CHIP = 24
HALO = 6
WIN = 18
PER_TILE = 7
FAR = 6
OPEN = 8
CAPACITY = 24
LEVELS = (24,)
SLOTS = CHIP + 2 * CAPACITY
GATHER_AT = 2 * CAPACITY
LEVEL_AT = GATHER_AT + PART


def plan_kernel(anc_ref, plan_ref, need, ranks, lists):
    member = lax.axis_index("member")
    chip = lax.div(member, 2)

    def third(a):
        return lax.shift_right_logical(a * 2731, 16)

    for i in range(4 * 96):
        need[i] = 0
    for j in range(96):
        need[(j // CHIP) * 96 + anc_ref[j]] = 1
    counts = {}
    for d in range(4):
        for k in range(1, 4):
            s = (d + k) % 4
            cnt = jnp.int32(0)
            for p in range(CHIP):
                v = need[d * 96 + s * CHIP + p]
                ranks[d * 96 + s * CHIP + p] = cnt
                lists[(d * 4 + k) * 32 + cnt] = p
                cnt = cnt + v
            counts[d, k] = cnt
    c1 = [counts[d, 1] for d in range(4)]
    c2 = [counts[d, 2] for d in range(4)]
    c3 = [counts[d, 3] for d in range(4)]

    def clamp(d, x):
        return jnp.minimum(jnp.maximum(x, jnp.maximum(0, c2[d] - FAR)), jnp.minimum(FAR, c2[d]))

    def worst(a):
        top = jnp.int32(0)
        for s in range(4):
            d1, d2, u1 = (s - 1) % 4, (s - 2) % 4, (s + 1) % 4
            down = jnp.maximum(OPEN, a[d2] + c1[d1]) + a[d1]
            up = jnp.maximum(OPEN, c2[d2] - a[d2] + c3[u1]) + c2[u1] - a[u1]
            top = jnp.maximum(top, jnp.maximum(down, up))
        return top

    a = [clamp(d, lax.shift_right_arithmetic(c2[d] + c3[d] - c1[d] + 1, 1)) for d in range(4)]
    for d in range(4):
        b = [c2[e] - a[e] for e in range(4)]

        def down(s):
            return a[(s - 2) % 4] + c1[(s - 1) % 4] + a[(s - 1) % 4]

        def up(s):
            return b[(s + 2) % 4] + c3[(s + 1) % 4] + b[(s + 1) % 4]

        m = jnp.maximum(down((d + 2) % 4), down((d + 1) % 4)) - a[d]
        n = jnp.maximum(up((d + 2) % 4), up((d + 3) % 4)) - b[d]
        a[d] = clamp(d, lax.shift_right_arithmetic(n + c2[d] - m + 1, 1))
    top = worst(a)
    half = [lax.shift_right_logical(c2[d] + 1, 1) for d in range(4)]
    fits = top <= CAPACITY
    a = [jnp.where(fits, a[d], half[d]) for d in range(4)]
    top = jnp.where(fits, top, CAPACITY)
    b = [c2[d] - a[d] for d in range(4)]

    def at(values, index):
        index = lax.rem(index + 8, 4)
        out = values[3]
        for i in range(3):
            out = jnp.where(index == i, values[i], out)
        return out

    def entry(row, i):
        v = lists[row + i]
        return jnp.minimum(jnp.maximum(v, 0), CHIP - 1)

    d1, d2, u1 = lax.rem(chip + 3, 4), lax.rem(chip + 2, 4), lax.rem(chip + 1, 4)
    far_row = (d2 * 4 + 2) * 32
    a_far, b_far = at(a, d2), at(b, d2)
    down_fwd = jnp.maximum(OPEN, a_far + at(c1, d1))
    up_fwd = jnp.maximum(OPEN, b_far + at(c3, u1))
    for i in range(CAPACITY):
        plan_ref[i] = 0
        plan_ref[CAPACITY + i] = 0
    for i in range(FAR):
        plan_ref[i] = entry(far_row, i)
        plan_ref[CAPACITY + i] = entry(far_row, a_far + i)
    for i in range(PART):
        plan_ref[a_far + i] = entry((d1 * 4 + 1) * 32, i)
        plan_ref[CAPACITY + b_far + i] = entry((u1 * 4 + 3) * 32, i)
    for i in range(FAR):
        plan_ref[down_fwd + i] = CHIP + i
        plan_ref[CAPACITY + up_fwd + i] = CHIP + i

    own_a = at(a, chip)
    from_up = at(a, chip + 3)
    from_down = at(b, chip + 1)
    far_down = jnp.maximum(OPEN, at(a, chip + 3) + at(c1, chip))
    far_up = jnp.maximum(OPEN, at(b, chip + 1) + at(c3, chip))
    for j in range(PART):
        old = anc_ref[member * PART + j]
        src = third(old)
        k = lax.rem(src - chip + 4, 4)
        r = ranks[chip * 96 + old]
        far = jnp.where(r < own_a, CHIP + far_down + r, CHIP + CAPACITY + far_up + r - own_a)
        where = jnp.where(
            k == 0,
            old - src * CHIP,
            jnp.where(
                k == 1,
                CHIP + from_up + r,
                jnp.where(k == 3, CHIP + CAPACITY + from_down + r, far),
            ),
        )
        plan_ref[GATHER_AT + j] = where
    level = jnp.int32(0)
    for size in LEVELS[:-1]:
        level = level + jnp.where(top > size, 1, 0)
    plan_ref[LEVEL_AT] = level


def make_plan(ancestors):
    return pl.pallas_call(
        plan_kernel,
        out_shape=jax.ShapeDtypeStruct((64,), jnp.int32),
        in_specs=[pl.BlockSpec(memory_space=pltpu.SMEM)],
        out_specs=pl.BlockSpec(memory_space=pltpu.SMEM),
        scratch_shapes=[
            pltpu.SMEM((4 * 96,), jnp.int32),
            pltpu.SMEM((4 * 96,), jnp.int32),
            pltpu.SMEM((16 * 32,), jnp.int32),
        ],
    )(ancestors)


def one_step(u, v, h, cor, obs, nud, force):
    rows, lanes = u.shape
    row = lax.broadcasted_iota(jnp.int32, u.shape, 0)

    def across(q):
        return pltpu.roll(q, lanes - 1, 1) - pltpu.roll(q, 1, 1)

    def along(q):
        above = jnp.where(row == rows - 1, 0.0, pltpu.roll(q, rows - 1, 0))
        below = jnp.where(row == 0, 0.0, pltpu.roll(q, 1, 0))
        return above - below

    u_new = u + cor * v - 0.125 * across(h)
    v_new = v - cor * u - 0.125 * along(h)
    h_new = h - 0.125 * (across(u_new) + along(v_new)) + nud * (obs - h) + force
    return u_new, v_new, h_new


def cycle_kernel(
    size, plan, ens_hbm, pert_hbm, obs_hbm, prec_hbm, nud_hbm, cor_hbm,
    slots, lw_out,
    ens, pert, fields, cor_v, pool, first, stage, msg_out, msg_in, win, edge,
    misfit, zbuf, xbuf, lwbuf,
    in_sem, const_sem, halo_send, halo_recv, pool_send, pool_recv,
    ring_send, ring_recv, mir_send, mir_recv, out_sem,
    z_send, z_recv, x_send, x_recv, m_send, m_recv,
):
    member, lon = lax.axis_index("member"), lax.axis_index("lon")
    core = lax.rem(member, 2)
    lon_x, lon_z = lax.div(lon, 4), lax.rem(lon, 4)
    sibling = {"member": member + 1 - 2 * core}
    ring = ({"member": lax.rem(member + 6, 8)}, {"member": lax.rem(member + 2, 8)})
    sides = ({"lon": lax.rem(lon + 15, 16)}, {"lon": lax.rem(lon + 1, 16)})
    z_peers = [{"lon": lon_x * 4 + lax.rem(lon_z + k, 4)} for k in range(1, 4)]
    x_peers = [{"lon": lax.rem(lon_x + k, 4) * 4 + lon_z} for k in range(1, 4)]
    m_peers = [{"member": lax.rem(member + k, 8)} for k in range(1, 8)]

    def remote(src, dst, ssem, rsem, to):
        return pltpu.make_async_remote_copy(
            src_ref=src, dst_ref=dst, send_sem=ssem, recv_sem=rsem, device_id=to, device_id_type=MESH
        )

    loads = []
    for g in range(3):
        part = pl.ds(4 * g, 4)
        loads.append((
            pltpu.make_async_copy(ens_hbm.at[part], ens.at[part], in_sem.at[0, g]),
            pltpu.make_async_copy(pert_hbm.at[part], pert.at[part], in_sem.at[1, g]),
        ))
    consts = [
        pltpu.make_async_copy(ref, fields.at[i], const_sem.at[i])
        for i, ref in enumerate((obs_hbm, prec_hbm, nud_hbm))
    ] + [pltpu.make_async_copy(cor_hbm, cor_v, const_sem.at[3])]
    for cp in consts:
        cp.start()
    for pair in loads:
        for cp in pair:
            cp.start()

    barrier = pltpu.get_barrier_semaphore()
    everyone = list(sides) + z_peers + x_peers + m_peers
    for peer in everyone:
        pl.semaphore_signal(barrier, inc=1, device_id=peer, device_id_type=MESH)

    for cp in consts:
        cp.wait()
    for pair in loads:
        for cp in pair:
            cp.wait()

    lane = lax.broadcasted_iota(jnp.int32, (LAT, 128), 1)

    def tile(which, p, side):
        cut = slice(0, 128) if side == 0 else slice(128, 256)
        if which < 3:
            return ens[p, which, :, cut]
        if which < 6:
            return pert[p, which - 3, :, cut]
        return fields[0 if which == 6 else 2, :, cut]

    def turned(x, by):
        by = by % 128
        return x if by == 0 else pltpu.roll(x, by, 1)

    def item(which, p):
        i = which * PART + p if which < 5 else (60 if which == 6 else 61)
        return i // 21, 6 * (i % 21)

    items = [(f, p) for f in range(5) for p in range(PART)] + [(6, 0), (7, 0)]
    for side in range(2):
        start = 0 if side == 0 else 122
        acc = [None] * 3
        for f, p in items:
            t, o = item(f, p)
            x = turned(tile(f, p, side), o - start)
            acc[t] = x if acc[t] is None else jnp.where(lane >= o, x, acc[t])
        for t in range(3):
            msg_out[side, t] = acc[t]

    pl.semaphore_wait(barrier, len(everyone))
    halos = [
        remote(msg_out.at[s], msg_in.at[1 - s], halo_send.at[s], halo_recv.at[1 - s], sides[s])
        for s in range(2)
    ]
    for cp in halos:
        cp.start()

    def interior(p, carry):
        cor = jnp.concatenate([cor_v[...], cor_v[...]], axis=1)
        u, v, h = ens[p, 0], ens[p, 1], ens[p, 2]
        for step in range(STEPS):
            u, v, h = one_step(u, v, h, cor, fields[0], fields[2], pert[p, step])
        at = core * PART + p
        pool[at, 0], pool[at, 1], pool[at, 2] = u, v, h
        return carry

    lax.fori_loop(0, PART, interior, 0)

    for s in range(2):
        remote(msg_out.at[s], msg_in.at[s], halo_send.at[s], halo_recv.at[s], sides[s]).wait_recv()
    for s in range(2):
        for half in range(2):
            members = list(range(half * PER_TILE, min(PART, (half + 1) * PER_TILE)))
            for f in range(8):
                if f >= 6 and half == 1:
                    continue
                count = PER_TILE if f >= 6 else len(members)
                acc = None
                for q in range(count):
                    p = members[q] if f < 6 else 0
                    o = WIN * q
                    if s == 0:
                        own, own_o = turned(tile(f, p, 0), o + HALO), o + HALO
                        nb_o = o
                    else:
                        own, own_o = turned(tile(f, p, 1), o - 116), o
                        nb_o = o + 2 * HALO
                    parts = [(own_o, own)]
                    if f != 5:
                        t, io = item(f, p)
                        nb = turned(msg_in[s, t], nb_o - io)
                        parts.append((nb_o, nb))
                    parts.sort(key=lambda e: e[0])
                    for off, x in parts:
                        acc = x if acc is None else jnp.where(lane >= off, x, acc)
                win[s, half, f] = acc
    for s in range(2):
        for half in range(2):
            u, v, h = win[s, half, 0], win[s, half, 1], win[s, half, 2]
            for step in range(STEPS):
                u, v, h = one_step(u, v, h, cor_v[...], win[s, 0, 6], win[s, 0, 7], win[s, half, 3 + step])
            edge[s, half, 0], edge[s, half, 1], edge[s, half, 2] = u, v, h

    shares = []
    for p in range(PART):
        at = core * PART + p
        half, q = p // PER_TILE, p % PER_TILE
        for f in range(3):
            left = turned(edge[0, half, f], -(WIN * q + HALO))
            right = turned(edge[1, half, f], 122 - (WIN * q + HALO))
            low = jnp.where(lane < HALO, left, pool[at, f, :, 0:128])
            high = jnp.where(lane >= 122, right, pool[at, f, :, 128:256])
            pool[at, f, :, 0:128] = low
            pool[at, f, :, 128:256] = high
        cp = remote(pool.at[at], pool.at[at], pool_send.at[p], pool_recv.at[p], sibling)
        cp.start()
        shares.append(cp)
        lo = fields[0, :, 0:128] - low
        hi = fields[0, :, 128:256] - high
        term = fields[1, :, 0:128] * lo * lo + fields[1, :, 128:256] * hi * hi
        misfit[p:p + 1, :] = jnp.sum(term, axis=0, keepdims=True)

    total = jnp.sum(misfit[...], axis=1, keepdims=True)
    small = lax.broadcasted_iota(jnp.int32, (PART, 128), 1)
    which = lax.broadcasted_iota(jnp.int32, (PART, 128), 0)
    line = jnp.sum(jnp.where(small == which, total, 0.0), axis=0, keepdims=True)
    zbuf[lon_z] = jnp.broadcast_to(line, (8, 128))
    z_copies = [
        remote(zbuf.at[lon_z], zbuf.at[lon_z], z_send.at[k], z_recv.at[k], z_peers[k]) for k in range(3)
    ]
    for cp in z_copies:
        cp.start()

    for p in range(PART):
        other = (1 - core) * PART + p
        remote(pool.at[other], pool.at[other], pool_send.at[p], pool_recv.at[p], sibling).wait_recv()
    keep = [pltpu.make_async_copy(pool, slots.at[pl.ds(0, CHIP)], out_sem.at[0])]
    keep[0].start()

    lanes_per_core = size // 2
    open_pos, far_pos = OPEN // 2, FAR // 2

    def landing(way, pos, on_core):
        i = 2 * pos + on_core
        if pos < far_pos:
            return first.at[way, i]
        return slots.at[CHIP + way * CAPACITY + i]

    def ring_copy(way, pos):
        return remote(
            stage.at[way, pos], landing(way, pos, core), ring_send.at[way, pos], ring_recv.at[way, pos], ring[way]
        )

    def mirror_copy(way, pos, on_core):
        ref = landing(way, pos, on_core)
        return remote(ref, ref, mir_send.at[way, pos], mir_recv.at[way, pos], sibling)

    for pos in range(open_pos):
        for way in range(2):
            stage[way, pos] = pool[plan[way * CAPACITY + 2 * pos + core]]
            ring_copy(way, pos).start()

    for k in range(3):
        z_copies[k].wait_send()
        z_copies[k].wait_recv()
    xbuf[lon_x] = ((zbuf[0] + zbuf[1]) + zbuf[2]) + zbuf[3]
    x_copies = [
        remote(xbuf.at[lon_x], xbuf.at[lon_x], x_send.at[k], x_recv.at[k], x_peers[k]) for k in range(3)
    ]
    for cp in x_copies:
        cp.start()
    for cp in x_copies:
        cp.wait_send()
        cp.wait_recv()
    lwbuf[member] = ((xbuf[0] + xbuf[1]) + xbuf[2]) + xbuf[3]
    m_copies = [
        remote(lwbuf.at[member], lwbuf.at[member], m_send.at[k], m_recv.at[k], m_peers[k]) for k in range(7)
    ]
    for cp in m_copies:
        cp.start()

    for pos in range(far_pos):
        for way in range(2):
            ring_copy(way, pos).wait_recv()
            mirror_copy(way, pos, core).start()
    for pos in range(far_pos):
        for way in range(2):
            mirror_copy(way, pos, 1 - core).wait_recv()
    for way in range(2):
        cp = pltpu.make_async_copy(
            first.at[way], slots.at[pl.ds(CHIP + way * CAPACITY, FAR)], out_sem.at[1 + way]
        )
        cp.start()
        keep.append(cp)
    for pos in range(open_pos, lanes_per_core):
        for way in range(2):
            idx = plan[way * CAPACITY + 2 * pos + core]
            own = pool[jnp.minimum(idx, CHIP - 1)]
            passed = first[way, jnp.clip(idx - CHIP, 0, FAR - 1)]
            stage[way, pos] = jnp.where(idx < CHIP, own, passed)
            ring_copy(way, pos).start()
    for pos in range(far_pos, lanes_per_core):
        for way in range(2):
            ring_copy(way, pos).wait_recv()
            mirror_copy(way, pos, core).start()

    for cp in m_copies:
        cp.wait_send()
        cp.wait_recv()
    lw_out[...] = lwbuf[...]
    for cp in halos + shares:
        cp.wait_send()
    for pos in range(lanes_per_core):
        for way in range(2):
            ring_copy(way, pos).wait_send()
    for pos in range(lanes_per_core):
        for way in range(2):
            mirror_copy(way, pos, core).wait_send()
            if pos >= far_pos:
                mirror_copy(way, pos, 1 - core).wait_recv()
    for cp in keep:
        cp.wait()


def run_cycle(size, number, plan, ensemble, perturbation, observed, precision, nudging, coriolis):
    anywhere = pl.BlockSpec(memory_space=pl.ANY)
    dma = pltpu.SemaphoreType.DMA
    most = size // 2
    return pl.pallas_call(
        functools.partial(cycle_kernel, size),
        out_shape=(
            jax.ShapeDtypeStruct((SLOTS, 3, LAT, CLON), F32),
            jax.ShapeDtypeStruct((8, 8, 128), F32),
        ),
        in_specs=[pl.BlockSpec(memory_space=pltpu.SMEM)] + [anywhere] * 6,
        out_specs=(anywhere, pl.BlockSpec(memory_space=pltpu.VMEM)),
        scratch_shapes=[
            pltpu.VMEM((PART, 3, LAT, CLON), F32),
            pltpu.VMEM((PART, 3, LAT, CLON), F32),
            pltpu.VMEM((3, LAT, CLON), F32),
            pltpu.VMEM((LAT, 128), F32),
            pltpu.VMEM((CHIP, 3, LAT, CLON), F32),
            pltpu.VMEM((2, FAR, 3, LAT, CLON), F32),
            pltpu.VMEM((2, most, 3, LAT, CLON), F32),
            pltpu.VMEM((2, 3, LAT, 128), F32),
            pltpu.VMEM((2, 3, LAT, 128), F32),
            pltpu.VMEM((2, 2, 8, LAT, 128), F32),
            pltpu.VMEM((2, 2, 3, LAT, 128), F32),
            pltpu.VMEM((PART, 128), F32),
            pltpu.VMEM((4, 8, 128), F32),
            pltpu.VMEM((4, 8, 128), F32),
            pltpu.VMEM((8, 8, 128), F32),
            dma((2, 3)), dma((4,)), dma((2,)), dma((2,)), dma((PART,)), dma((PART,)),
            dma((2, most)), dma((2, most)), dma((2, most)), dma((2, most)), dma((3,)),
            dma((3,)), dma((3,)), dma((3,)), dma((3,)), dma((7,)), dma((7,)),
        ],
        compiler_params=pltpu.CompilerParams(
            collective_id=number, has_side_effects=True, vmem_limit_bytes=50 * 2**20
        ),
    )(plan, ensemble, perturbation, observed, precision, nudging, coriolis)


def resample_kernel(plan, lw_ref, slots, weights_ref, analysis, sems):
    copies = [
        pltpu.make_async_copy(slots.at[plan[GATHER_AT + j]], analysis.at[j], sems.at[j]) for j in range(PART)
    ]
    for cp in copies:
        cp.start()
    lane = lax.broadcasted_iota(jnp.int32, (8, 8, 128), 2)
    logw = jnp.where(lane < PART, lw_ref[...] * (-2.0 / (LAT * CLON * 16)), -jnp.inf)
    top = jnp.max(jnp.max(logw, axis=0), axis=1, keepdims=True)
    e = jnp.exp(logw - top[None])
    whole = jnp.sum(jnp.sum(e, axis=0), axis=1, keepdims=True)
    own = jnp.where(
        lax.broadcasted_iota(jnp.int32, (8, 8, 128), 0) == lax.axis_index("member"), e, 0.0
    )
    row = jnp.sum(own, axis=0) / whole
    weights_ref[...] = row[0, :PART]
    for cp in copies:
        cp.wait()


def resample(plan, lw, slots):
    return pl.pallas_call(
        resample_kernel,
        out_shape=(
            jax.ShapeDtypeStruct((PART,), F32),
            jax.ShapeDtypeStruct((PART, 3, LAT, CLON), F32),
        ),
        in_specs=[
            pl.BlockSpec(memory_space=pltpu.SMEM),
            pl.BlockSpec(memory_space=pltpu.VMEM),
            pl.BlockSpec(memory_space=pl.ANY),
        ],
        out_specs=(pl.BlockSpec(memory_space=pltpu.VMEM), pl.BlockSpec(memory_space=pl.ANY)),
        scratch_shapes=[pltpu.SemaphoreType.DMA((PART,))],
    )(plan, lw, slots)


def body(ensemble, perturbation, observed, precision, nudging, ancestors):
    rows = np.arange(LAT).astype(np.float32)
    cor = (0.3 * np.sin(np.float32(math.pi) * (rows + np.float32(0.5 - LAT / 2)) / np.float32(LAT))).astype(np.float32)
    coriolis = jnp.asarray(np.broadcast_to(cor[:, None], (LAT, 128)))
    plan = make_plan(ancestors)
    operands = (plan, ensemble, perturbation, observed, precision, nudging, coriolis)
    branches = [functools.partial(run_cycle, size, n) for n, size in enumerate(LEVELS)]
    if len(branches) == 1:
        slots, lw = branches[0](*operands)
    else:
        slots, lw = lax.switch(plan[LEVEL_AT], branches, *operands)
    weights, analysis = resample(plan, lw, slots)
    return weights, analysis


def solution(mesh):
    placed = (
        P("member", None, None, "lon"),
        P("member", None, None, "lon"),
        P(None, "lon"),
        P(None, "lon"),
        P(None, "lon"),
        P(),
    )
    return jax.shard_map(
        body,
        mesh=mesh,
        in_specs=placed,
        out_specs=(P("member"), P("member", None, None, "lon")),
        check_vma=False,
    )
```

time: 219 us -> 166 us (0.76)
  Pallas kernels: 0 us -> 159 us
  waiting for transfers between devices: 96.8 us -> 0 us
  blocking collectives: 55 us -> 0 us
  matrix products: 21.5 us -> 0 us
  starting transfers between devices: 14.6 us -> 0 us
  between operations: 14.8 us -> 0.66 us
  other arithmetic: 8.9 us -> 0 us
    pallas_call x0 -> x3, Pallas kernels: none -> 159 us  [the longest x1 82.5 us: run_cycle(): pl.pallas_call(functools.partial(cycle_kernel, size), out_shape=(jax.Shap...]
    ppermute x12 -> x0, waiting for transfers between devices: 60.3 us -> none  [the longest x6 37.2 us: with_halo(): after = lax.ppermute(first, axis, down)]
    all_gather x1 -> x0, waiting for transfers between devices: 36.5 us -> none  [body(): piece = lax.all_gather(state, 'member', axis=0, tiled=True)]
    psum x1 -> x0, blocking collectives: 28.5 us -> none  [body(): weight_totals = lax.psum(partial_sum, 'lon')]
    unnamed x1 -> x0, blocking collectives: 26.5 us -> none
    dot_general x1 -> x0, matrix products: 21.5 us -> none  [body(): jnp.einsum('jn,nfyx->jfyx', select, piece, precision=lax.Precision.HIGHEST)]
    ppermute x12 -> x0, starting transfers between devices: 14.5 us -> none  [the longest x6 8.38 us: with_halo(): after = lax.ppermute(first, axis, down)]
    unnamed x17 -> x12, local copies, waits for them, and re-layouts: 4.01 us -> 5.47 us
  transfers between devices with their start and end apart: 13 -> 0, of which waited for: 13 -> 0; matrix products, arithmetic and copies ran while one was open for 2% -> 0% of each run, Pallas kernels for 0% -> 0%
where the time goes in v1:
time: 166 us
  Pallas kernels  159 us (96%)
  local copies, waits for them, and re-layouts  6.19 us (4%)
    pallas_call x1, Pallas kernels, run_cycle(): pl.pallas_call(functools.partial(cycle_kernel, size), out_shape=(jax.Shap...  82.5 us
    pallas_call x1, Pallas kernels, resample(): pl.pallas_call(resample_kernel, out_shape=(jax.ShapeDtypeStruct((PART,),...  74 us
    unnamed x12, local copies, waits for them, and re-layouts  5.47 us

profile of v1, /device:TPU:1, one launch (start us, length us, event | category | flops | bytes accessed | tf_op | source)
XLA Modules:
  0.0 165.6 jit_solution(14495754282496146794)
XLA Ops:
  0.6 2.3 %shard_map.86.plan = s32[64]{0:T(128)} custom-call(s32[96]{0:T(128)} %anc_ref.1), custom_call_target="tpu_custom_call" | custom-call | tf_op jit(solution)/shard_map/pallas_call | solution.py:146
  2.9 0.7 jit_solution_.3.cor_hbm
  3.7 0.0 copy-start
  3.7 1.7 %copy-done = f32[12,3,64,256]{3,2,1,0:T(8,128)S(1)} copy-done((f32[12,3,64,256]{3,2,1,0:T(8,128)S(1)}, f32[12,3,64,256]{3,2,1,0:T(8,128)}, u32[]{:S(2)}) %copy-start) | copy-done | bytes 2359320
  5.3 0.0 copy-start.1
  5.3 0.8 copy-done.1
  6.2 0.0 copy-start.2
  6.2 0.8 copy-done.2
  7.0 0.0 copy-start.3
  7.0 0.8 copy-done.3
  7.9 0.0 copy-start.5
  7.9 0.7 copy-done.5
  8.5 82.5 %shard_map.87 = (f32[72,3,64,256]{3,2,1,0:T(8,128)}, f32[8,8,128]{2,1,0:T(8,128)S(1)}) custom-call(s32[64]{0:T(128)S(1)} %copy-done.5, f32[12,3,64,256]{3,2,1,0:T(8,128)S(1)} %copy-done, f32[12,3,64,256]{3,2,1,0:T(8,128)} %pert_hbm.1, f32[64,256]{1,0:T(8,128)S(1)} %copy-done.1, f32[64,256]{1,0:T(8,128)S(1)} %copy-done.2, f32[64,256]{1,0:T(8,128)S(1)} %copy-done.3, ...), custom_call_target="tpu_custom_call" | custom-call | tf_op jit(solution)/shard_map/pallas_call | solution.py:437
  91.0 0.0 copy-start.4
  91.0 0.6 copy-done.4
  91.7 74.0 %shard_map.88 = (f32[12]{0:T(128)}, f32[12,3,64,256]{3,2,1,0:T(8,128)}) custom-call(s32[64]{0:T(128)} %shard_map.86.plan, f32[8,8,128]{2,1,0:T(8,128)} %copy-done.4, f32[72,3,64,256]{3,2,1,0:T(8,128)} %get-tuple-element.5.slots), custom_call_target="tpu_custom_call" | custom-call | tf_op jit(solution)/shard_map/pallas_call | solution.py:492
Async XLA Ops:
  3.7 1.7 %copy-start = (f32[12,3,64,256]{3,2,1,0:T(8,128)S(1)}, f32[12,3,64,256]{3,2,1,0:T(8,128)}, u32[]{:S(2)}) copy-start(f32[12,3,64,256]{3,2,1,0:T(8,128)} %ens_hbm.1) | copy-start | bytes 7077892
  5.3 0.8 copy-start.1
  6.2 0.8 copy-start.2
  7.0 0.8 copy-start.3
  7.9 0.7 copy-start.5
  91.0 0.6 copy-start.4

commit v2 on v1

--- a/solution.py
+++ b/solution.py
@@ -3,7 +3,6 @@
 
 import jax
 import jax.numpy as jnp
-import numpy as np
 from jax import lax
 from jax.experimental import pallas as pl
 from jax.experimental.pallas import tpu as pltpu
@@ -22,7 +21,7 @@
 FAR = 6
 OPEN = 8
 CAPACITY = 24
-LEVELS = (24,)
+LEVELS = (12, 14, 24)
 SLOTS = CHIP + 2 * CAPACITY
 GATHER_AT = 2 * CAPACITY
 LEVEL_AT = GATHER_AT + PART
@@ -175,7 +174,7 @@
 
 
 def cycle_kernel(
-    size, plan, ens_hbm, pert_hbm, obs_hbm, prec_hbm, nud_hbm, cor_hbm,
+    size, plan, ens_hbm, pert_hbm, obs_hbm, prec_hbm, nud_hbm,
     slots, lw_out,
     ens, pert, fields, cor_v, pool, first, stage, msg_out, msg_in, win, edge,
     misfit, zbuf, xbuf, lwbuf,
@@ -208,7 +207,7 @@
     consts = [
         pltpu.make_async_copy(ref, fields.at[i], const_sem.at[i])
         for i, ref in enumerate((obs_hbm, prec_hbm, nud_hbm))
-    ] + [pltpu.make_async_copy(cor_hbm, cor_v, const_sem.at[3])]
+    ]
     for cp in consts:
         cp.start()
     for pair in loads:
@@ -219,6 +218,9 @@
     everyone = list(sides) + z_peers + x_peers + m_peers
     for peer in everyone:
         pl.semaphore_signal(barrier, inc=1, device_id=peer, device_id_type=MESH)
+
+    row_at = lax.broadcasted_iota(jnp.int32, (LAT, 128), 0).astype(F32)
+    cor_v[...] = 0.3 * jnp.sin(math.pi * (row_at + 0.5 - LAT / 2) / LAT)
 
     for cp in consts:
         cp.wait()
@@ -430,8 +432,8 @@
         cp.wait()
 
 
-def run_cycle(size, number, plan, ensemble, perturbation, observed, precision, nudging, coriolis):
-    anywhere = pl.BlockSpec(memory_space=pl.ANY)
+def run_cycle(size, number, plan, ensemble, perturbation, observed, precision, nudging):
+    anywhere = pl.BlockSpec(memory_space=pltpu.HBM)
     dma = pltpu.SemaphoreType.DMA
     most = size // 2
     return pl.pallas_call(
@@ -440,7 +442,7 @@
             jax.ShapeDtypeStruct((SLOTS, 3, LAT, CLON), F32),
             jax.ShapeDtypeStruct((8, 8, 128), F32),
         ),
-        in_specs=[pl.BlockSpec(memory_space=pltpu.SMEM)] + [anywhere] * 6,
+        in_specs=[pl.BlockSpec(memory_space=pltpu.SMEM)] + [anywhere] * 5,
         out_specs=(anywhere, pl.BlockSpec(memory_space=pltpu.VMEM)),
         scratch_shapes=[
             pltpu.VMEM((PART, 3, LAT, CLON), F32),
@@ -458,21 +460,22 @@
             pltpu.VMEM((4, 8, 128), F32),
             pltpu.VMEM((4, 8, 128), F32),
             pltpu.VMEM((8, 8, 128), F32),
-            dma((2, 3)), dma((4,)), dma((2,)), dma((2,)), dma((PART,)), dma((PART,)),
+            dma((2, 3)), dma((3,)), dma((2,)), dma((2,)), dma((PART,)), dma((PART,)),
             dma((2, most)), dma((2, most)), dma((2, most)), dma((2, most)), dma((3,)),
             dma((3,)), dma((3,)), dma((3,)), dma((3,)), dma((7,)), dma((7,)),
         ],
         compiler_params=pltpu.CompilerParams(
             collective_id=number, has_side_effects=True, vmem_limit_bytes=50 * 2**20
         ),
-    )(plan, ensemble, perturbation, observed, precision, nudging, coriolis)
-
-
-def resample_kernel(plan, lw_ref, slots, weights_ref, analysis, sems):
-    copies = [
-        pltpu.make_async_copy(slots.at[plan[GATHER_AT + j]], analysis.at[j], sems.at[j]) for j in range(PART)
+    )(plan, ensemble, perturbation, observed, precision, nudging)
+
+
+def resample_kernel(plan, lw_ref, slots, weights_ref, analysis, held, in_sem, out_sem):
+    ins = [
+        pltpu.make_async_copy(slots.at[plan[GATHER_AT + j]], held.at[j], in_sem.at[j]) for j in range(PART)
     ]
-    for cp in copies:
+    outs = [pltpu.make_async_copy(held.at[j], analysis.at[j], out_sem.at[j]) for j in range(PART)]
+    for cp in ins:
         cp.start()
     lane = lax.broadcasted_iota(jnp.int32, (8, 8, 128), 2)
     logw = jnp.where(lane < PART, lw_ref[...] * (-2.0 / (LAT * CLON * 16)), -jnp.inf)
@@ -484,7 +487,10 @@
     )
     row = jnp.sum(own, axis=0) / whole
     weights_ref[...] = row[0, :PART]
-    for cp in copies:
+    for j in range(PART):
+        ins[j].wait()
+        outs[j].start()
+    for cp in outs:
         cp.wait()
 
 
@@ -498,19 +504,20 @@
         in_specs=[
             pl.BlockSpec(memory_space=pltpu.SMEM),
             pl.BlockSpec(memory_space=pltpu.VMEM),
-            pl.BlockSpec(memory_space=pl.ANY),
+            pl.BlockSpec(memory_space=pltpu.HBM),
         ],
-        out_specs=(pl.BlockSpec(memory_space=pltpu.VMEM), pl.BlockSpec(memory_space=pl.ANY)),
-        scratch_shapes=[pltpu.SemaphoreType.DMA((PART,))],
+        out_specs=(pl.BlockSpec(memory_space=pltpu.VMEM), pl.BlockSpec(memory_space=pltpu.HBM)),
+        scratch_shapes=[
+            pltpu.VMEM((PART, 3, LAT, CLON), F32),
+            pltpu.SemaphoreType.DMA((PART,)),
+            pltpu.SemaphoreType.DMA((PART,)),
+        ],
     )(plan, lw, slots)
 
 
 def body(ensemble, perturbation, observed, precision, nudging, ancestors):
-    rows = np.arange(LAT).astype(np.float32)
-    cor = (0.3 * np.sin(np.float32(math.pi) * (rows + np.float32(0.5 - LAT / 2)) / np.float32(LAT))).astype(np.float32)
-    coriolis = jnp.asarray(np.broadcast_to(cor[:, None], (LAT, 128)))
     plan = make_plan(ancestors)
-    operands = (plan, ensemble, perturbation, observed, precision, nudging, coriolis)
+    operands = (plan, ensemble, perturbation, observed, precision, nudging)
     branches = [functools.partial(run_cycle, size, n) for n, size in enumerate(LEVELS)]
     if len(branches) == 1:
         slots, lw = branches[0](*operands)

time: 166 us -> 69.7 us (0.42)
  Pallas kernels: 159 us -> 66.8 us
  local copies, waits for them, and re-layouts: 6.19 us -> 0.58 us
    pallas_call x1, Pallas kernels: 74 us -> 3.68 us  [resample(): pl.pallas_call(resample_kernel, out_shape=(jax.ShapeDtypeStruct((PART,),...]
    pallas_call x1, Pallas kernels: 82.5 us -> 60.7 us  [run_cycle(): pl.pallas_call(functools.partial(cycle_kernel, size), out_shape=(jax.Shap...]
    unnamed x12 -> x0, local copies, waits for them, and re-layouts: 5.47 us -> none
where the time goes in v2:
time: 69.7 us; the launch traced here: 69.5 us
  Pallas kernels  66.8 us (96%)
  between operations  1.5 us (2%)
    pallas_call x1, Pallas kernels, run_cycle(): pl.pallas_call(functools.partial(cycle_kernel, size), out_shape=(jax.Shap...  60.7 us
    pallas_call x1, Pallas kernels, resample(): pl.pallas_call(resample_kernel, out_shape=(jax.ShapeDtypeStruct((PART,),...  3.68 us
    pallas_call x1, Pallas kernels, make_plan(): pl.pallas_call(plan_kernel, out_shape=jax.ShapeDtypeStruct((64,), jnp.int...  2.37 us

profile of v2, /device:TPU:1, one launch (start us, length us, event | category | flops | bytes accessed | tf_op | source)
XLA Modules:
  0.0 69.5 jit_solution(14796813931108732372)
XLA Ops:
  0.6 2.4 %shard_map.77.plan = s32[64]{0:T(128)S(1)} custom-call(s32[96]{0:T(128)} %anc_ref.1), custom_call_target="tpu_custom_call" | custom-call | tf_op jit(solution)/shard_map/pallas_call | solution.py:145
  3.0 0.6 slice.3
  4.2 61.4 %conditional.1 = ((f32[72,3,64,256]{3,2,1,0:T(8,128)}, f32[8,8,128]{2,1,0:T(8,128)S(1)})) conditional(s32[]{:T(128)} %bitcast, (s32[64]{0:T(128)S(1)}, f32[12,3,64,256]{3,2,1,0:T(8,128)}, f32[12,3,64,256]{3,2,1,0:T(8,128)}, f32[64,256]{1,0:T(8,128)}, f32[64,256]{1,0:T(8,128)}, /*index=5*/f32[64,256]{1,0:T(8,128)}) %tuple.16, ...), branch_computations={%region_0.0_spmd, %region_1.0_spmd, %region_2.0_spmd} | conditional | bytes 8 | solution.py:525
  4.5 60.7 %branch_1_fun.1 = (f32[72,3,64,256]{3,2,1,0:T(8,128)}, f32[8,8,128]{2,1,0:T(8,128)S(1)}) custom-call(s32[64]{0:T(128)S(1)} %get-tuple-element.42.plan, f32[12,3,64,256]{3,2,1,0:T(8,128)} %get-tuple-element.43.ens_hbm, f32[12,3,64,256]{3,2,1,0:T(8,128)} %get-tuple-element.44.pert_hbm, f32[64,256]{1,0:T(8,128)} %get-tuple-element.45.obs_hbm, ...), custom_call_target="tpu_custom_call" | custom-call | tf_op jit(solution)/shard_map/cond/branch_1_fun/pallas_call | solution.py:439
  65.7 3.7 %shard_map.78 = (f32[12]{0:T(128)}, f32[12,3,64,256]{3,2,1,0:T(8,128)}) custom-call(s32[64]{0:T(128)S(1)} %shard_map.77.plan, f32[8,8,128]{2,1,0:T(8,128)S(1)} %get-tuple-element.58.lw_ref, f32[72,3,64,256]{3,2,1,0:T(8,128)} %get-tuple-element.59.slots), custom_call_target="tpu_custom_call" | custom-call | tf_op jit(solution)/shard_map/pallas_call | solution.py:498

commit v3 on v2

--- a/solution.py
+++ b/solution.py
@@ -21,13 +21,12 @@
 FAR = 6
 OPEN = 8
 CAPACITY = 24
-LEVELS = (12, 14, 24)
+LEVELS = (12, 13, 14, 16, 24)
 SLOTS = CHIP + 2 * CAPACITY
 GATHER_AT = 2 * CAPACITY
-LEVEL_AT = GATHER_AT + PART
-
-
-def plan_kernel(anc_ref, plan_ref, need, ranks, lists):
+
+
+def plan_kernel(anc_ref, plan_ref, level_ref, need, ranks, lists):
     member = lax.axis_index("member")
     chip = lax.div(member, 2)
 
@@ -138,15 +137,15 @@
     level = jnp.int32(0)
     for size in LEVELS[:-1]:
         level = level + jnp.where(top > size, 1, 0)
-    plan_ref[LEVEL_AT] = level
+    level_ref[0] = level
 
 
 def make_plan(ancestors):
     return pl.pallas_call(
         plan_kernel,
-        out_shape=jax.ShapeDtypeStruct((64,), jnp.int32),
+        out_shape=(jax.ShapeDtypeStruct((64,), jnp.int32), jax.ShapeDtypeStruct((1,), jnp.int32)),
         in_specs=[pl.BlockSpec(memory_space=pltpu.SMEM)],
-        out_specs=pl.BlockSpec(memory_space=pltpu.SMEM),
+        out_specs=(pl.BlockSpec(memory_space=pltpu.SMEM), pl.BlockSpec(memory_space=pltpu.SMEM)),
         scratch_shapes=[
             pltpu.SMEM((4 * 96,), jnp.int32),
             pltpu.SMEM((4 * 96,), jnp.int32),
@@ -179,7 +178,7 @@
     ens, pert, fields, cor_v, pool, first, stage, msg_out, msg_in, win, edge,
     misfit, zbuf, xbuf, lwbuf,
     in_sem, const_sem, halo_send, halo_recv, pool_send, pool_recv,
-    ring_send, ring_recv, mir_send, mir_recv, out_sem,
+    edge_sem, ring_send, ring_recv, mir_send, mir_recv, out_sem,
     z_send, z_recv, x_send, x_recv, m_send, m_recv,
 ):
     member, lon = lax.axis_index("member"), lax.axis_index("lon")
@@ -265,6 +264,9 @@
     for cp in halos:
         cp.start()
 
+    def share(at, p):
+        return remote(pool.at[at], pool.at[at], pool_send.at[p], pool_recv.at[p], sibling)
+
     def interior(p, carry):
         cor = jnp.concatenate([cor_v[...], cor_v[...]], axis=1)
         u, v, h = ens[p, 0], ens[p, 1], ens[p, 2]
@@ -272,6 +274,7 @@
             u, v, h = one_step(u, v, h, cor, fields[0], fields[2], pert[p, step])
         at = core * PART + p
         pool[at, 0], pool[at, 1], pool[at, 2] = u, v, h
+        share(at, p).start()
         return carry
 
     lax.fori_loop(0, PART, interior, 0)
@@ -309,28 +312,81 @@
             u, v, h = win[s, half, 0], win[s, half, 1], win[s, half, 2]
             for step in range(STEPS):
                 u, v, h = one_step(u, v, h, cor_v[...], win[s, 0, 6], win[s, 0, 7], win[s, half, 3 + step])
-            edge[s, half, 0], edge[s, half, 1], edge[s, half, 2] = u, v, h
-
-    shares = []
+            edge[core, s, half, 0], edge[core, s, half, 1], edge[core, s, half, 2] = u, v, h
+
+    edge_copy = remote(edge.at[core], edge.at[core], edge_sem.at[0], edge_sem.at[1], sibling)
+    edge_copy.start()
     for p in range(PART):
-        at = core * PART + p
-        half, q = p // PER_TILE, p % PER_TILE
+        share((1 - core) * PART + p, p).wait_recv()
+    remote(edge.at[1 - core], edge.at[1 - core], edge_sem.at[0], edge_sem.at[1], sibling).wait_recv()
+
+    def whole(i):
+        on = jnp.where(i >= PART, 1, 0)
+        p = i - on * PART
+        half = jnp.where(p >= PER_TILE, 1, 0)
+        back = 128 - HALO - WIN * (p - half * PER_TILE)
+        out = []
         for f in range(3):
-            left = turned(edge[0, half, f], -(WIN * q + HALO))
-            right = turned(edge[1, half, f], 122 - (WIN * q + HALO))
-            low = jnp.where(lane < HALO, left, pool[at, f, :, 0:128])
-            high = jnp.where(lane >= 122, right, pool[at, f, :, 128:256])
-            pool[at, f, :, 0:128] = low
-            pool[at, f, :, 128:256] = high
-        cp = remote(pool.at[at], pool.at[at], pool_send.at[p], pool_recv.at[p], sibling)
-        cp.start()
-        shares.append(cp)
-        lo = fields[0, :, 0:128] - low
-        hi = fields[0, :, 128:256] - high
+            left = pltpu.roll(edge[on, 0, half, f], back, 1)
+            right = pltpu.roll(edge[on, 1, half, f], back - HALO, 1)
+            low = jnp.where(lane < HALO, left, pool[i, f, :, 0:128])
+            high = jnp.where(lane >= 128 - HALO, right, pool[i, f, :, 128:256])
+            out.append((low, high))
+        return out
+
+    positions = (size + 1) // 2
+    open_pos, far_pos = OPEN // 2, FAR // 2
+
+    def split(pos):
+        return 2 * pos + 1 == size
+
+    def entry_at(pos, on_core):
+        return 2 * pos if split(pos) else 2 * pos + on_core
+
+    def rows(ref, pos, on_core):
+        return ref.at[:, pl.ds(on_core * (LAT // 2), LAT // 2), :] if split(pos) else ref
+
+    def landing(way, pos, on_core):
+        i = entry_at(pos, on_core)
+        if pos < far_pos:
+            return first.at[way, i]
+        return rows(slots.at[CHIP + way * CAPACITY + i], pos, on_core)
+
+    def ring_copy(way, pos):
+        return remote(
+            rows(stage.at[way, pos], pos, core), landing(way, pos, core),
+            ring_send.at[way, pos], ring_recv.at[way, pos], ring[way],
+        )
+
+    def mirror_copy(way, pos, on_core):
+        ref = landing(way, pos, on_core)
+        return remote(ref, ref, mir_send.at[way, pos], mir_recv.at[way, pos], sibling)
+
+    for pos in range(open_pos):
+        for way in range(2):
+            parts = whole(plan[way * CAPACITY + entry_at(pos, core)])
+            for f in range(3):
+                stage[way, pos, f, :, 0:128], stage[way, pos, f, :, 128:256] = parts[f]
+            ring_copy(way, pos).start()
+
+    for p in range(PART):
+        share(core * PART + p, p).wait_send()
+
+    def complete(i, carry):
+        parts = whole(i)
+        for f in range(3):
+            pool[i, f, :, 0:128], pool[i, f, :, 128:256] = parts[f]
+        lo = fields[0, :, 0:128] - parts[2][0]
+        hi = fields[0, :, 128:256] - parts[2][1]
         term = fields[1, :, 0:128] * lo * lo + fields[1, :, 128:256] * hi * hi
-        misfit[p:p + 1, :] = jnp.sum(term, axis=0, keepdims=True)
-
-    total = jnp.sum(misfit[...], axis=1, keepdims=True)
+        misfit[i] = jnp.sum(term.reshape(LAT // 8, 8, 128), axis=0)
+        return carry
+
+    lax.fori_loop(0, CHIP, complete, 0)
+    keep = [pltpu.make_async_copy(pool, slots.at[pl.ds(0, CHIP)], out_sem.at[0])]
+    keep[0].start()
+
+    total = jnp.sum(jnp.sum(misfit[pl.ds(core * PART, PART)], axis=1), axis=1, keepdims=True)
     small = lax.broadcasted_iota(jnp.int32, (PART, 128), 1)
     which = lax.broadcasted_iota(jnp.int32, (PART, 128), 0)
     line = jnp.sum(jnp.where(small == which, total, 0.0), axis=0, keepdims=True)
@@ -341,35 +397,6 @@
     for cp in z_copies:
         cp.start()
 
-    for p in range(PART):
-        other = (1 - core) * PART + p
-        remote(pool.at[other], pool.at[other], pool_send.at[p], pool_recv.at[p], sibling).wait_recv()
-    keep = [pltpu.make_async_copy(pool, slots.at[pl.ds(0, CHIP)], out_sem.at[0])]
-    keep[0].start()
-
-    lanes_per_core = size // 2
-    open_pos, far_pos = OPEN // 2, FAR // 2
-
-    def landing(way, pos, on_core):
-        i = 2 * pos + on_core
-        if pos < far_pos:
-            return first.at[way, i]
-        return slots.at[CHIP + way * CAPACITY + i]
-
-    def ring_copy(way, pos):
-        return remote(
-            stage.at[way, pos], landing(way, pos, core), ring_send.at[way, pos], ring_recv.at[way, pos], ring[way]
-        )
-
-    def mirror_copy(way, pos, on_core):
-        ref = landing(way, pos, on_core)
-        return remote(ref, ref, mir_send.at[way, pos], mir_recv.at[way, pos], sibling)
-
-    for pos in range(open_pos):
-        for way in range(2):
-            stage[way, pos] = pool[plan[way * CAPACITY + 2 * pos + core]]
-            ring_copy(way, pos).start()
-
     for k in range(3):
         z_copies[k].wait_send()
         z_copies[k].wait_recv()
@@ -402,14 +429,14 @@
         )
         cp.start()
         keep.append(cp)
-    for pos in range(open_pos, lanes_per_core):
-        for way in range(2):
-            idx = plan[way * CAPACITY + 2 * pos + core]
+    for pos in range(open_pos, positions):
+        for way in range(2):
+            idx = plan[way * CAPACITY + entry_at(pos, core)]
             own = pool[jnp.minimum(idx, CHIP - 1)]
             passed = first[way, jnp.clip(idx - CHIP, 0, FAR - 1)]
             stage[way, pos] = jnp.where(idx < CHIP, own, passed)
             ring_copy(way, pos).start()
-    for pos in range(far_pos, lanes_per_core):
+    for pos in range(far_pos, positions):
         for way in range(2):
             ring_copy(way, pos).wait_recv()
             mirror_copy(way, pos, core).start()
@@ -418,12 +445,12 @@
         cp.wait_send()
         cp.wait_recv()
     lw_out[...] = lwbuf[...]
-    for cp in halos + shares:
+    for cp in halos + [edge_copy]:
         cp.wait_send()
-    for pos in range(lanes_per_core):
+    for pos in range(positions):
         for way in range(2):
             ring_copy(way, pos).wait_send()
-    for pos in range(lanes_per_core):
+    for pos in range(positions):
         for way in range(2):
             mirror_copy(way, pos, core).wait_send()
             if pos >= far_pos:
@@ -435,7 +462,7 @@
 def run_cycle(size, number, plan, ensemble, perturbation, observed, precision, nudging):
     anywhere = pl.BlockSpec(memory_space=pltpu.HBM)
     dma = pltpu.SemaphoreType.DMA
-    most = size // 2
+    most = (size + 1) // 2
     return pl.pallas_call(
         functools.partial(cycle_kernel, size),
         out_shape=(
@@ -455,12 +482,12 @@
             pltpu.VMEM((2, 3, LAT, 128), F32),
             pltpu.VMEM((2, 3, LAT, 128), F32),
             pltpu.VMEM((2, 2, 8, LAT, 128), F32),
-            pltpu.VMEM((2, 2, 3, LAT, 128), F32),
-            pltpu.VMEM((PART, 128), F32),
+            pltpu.VMEM((2, 2, 2, 3, LAT, 128), F32),
+            pltpu.VMEM((CHIP, 8, 128), F32),
             pltpu.VMEM((4, 8, 128), F32),
             pltpu.VMEM((4, 8, 128), F32),
             pltpu.VMEM((8, 8, 128), F32),
-            dma((2, 3)), dma((3,)), dma((2,)), dma((2,)), dma((PART,)), dma((PART,)),
+            dma((2, 3)), dma((3,)), dma((2,)), dma((2,)), dma((PART,)), dma((PART,)), dma((2,)),
             dma((2, most)), dma((2, most)), dma((2, most)), dma((2, most)), dma((3,)),
             dma((3,)), dma((3,)), dma((3,)), dma((3,)), dma((7,)), dma((7,)),
         ],
@@ -516,13 +543,13 @@
 
 
 def body(ensemble, perturbation, observed, precision, nudging, ancestors):
-    plan = make_plan(ancestors)
+    plan, level = make_plan(ancestors)
     operands = (plan, ensemble, perturbation, observed, precision, nudging)
     branches = [functools.partial(run_cycle, size, n) for n, size in enumerate(LEVELS)]
     if len(branches) == 1:
         slots, lw = branches[0](*operands)
     else:
-        slots, lw = lax.switch(plan[LEVEL_AT], branches, *operands)
+        slots, lw = lax.switch(level.reshape(()), branches, *operands)
     weights, analysis = resample(plan, lw, slots)
     return weights, analysis
 

time: 69.7 us -> 63.9 us (0.917)
  Pallas kernels: 66.8 us -> 61.5 us
    pallas_call x1, Pallas kernels: 60.7 us -> 55.4 us  [run_cycle(): pl.pallas_call(functools.partial(cycle_kernel, size), out_shape=(jax.Shap...]
where the time goes in v3:
time: 63.9 us; the launch traced here: 63.8 us
  Pallas kernels  61.5 us (96%)
  between operations  1.51 us (2%)
  loops' own time  0.73 us (1%)
    pallas_call x1, Pallas kernels, run_cycle(): pl.pallas_call(functools.partial(cycle_kernel, size), out_shape=(jax.Shap...  55.4 us
    pallas_call x1, Pallas kernels, resample(): pl.pallas_call(resample_kernel, out_shape=(jax.ShapeDtypeStruct((PART,),...  3.68 us
    pallas_call x1, Pallas kernels, make_plan(): pl.pallas_call(plan_kernel, out_shape=(jax.ShapeDtypeStruct((64,), jnp.in...  2.38 us

profile of v3, /device:TPU:1, one launch (start us, length us, event | category | flops | bytes accessed | tf_op | source)
XLA Modules:
  0.0 63.8 jit_solution(3907529333066654191)
XLA Ops:
  0.6 2.4 %shard_map.77 = (s32[64]{0:T(128)S(1)}, s32[1]{0:T(128)}) custom-call(s32[96]{0:T(128)} %anc_ref.1), custom_call_target="tpu_custom_call" | custom-call | tf_op jit(solution)/shard_map/pallas_call | solution.py:144
  3.7 56.2 %conditional.1 = ((f32[72,3,64,256]{3,2,1,0:T(8,128)}, f32[8,8,128]{2,1,0:T(8,128)S(1)})) conditional(s32[]{:T(128)} %bitcast, (s32[64]{0:T(128)S(1)}, f32[12,3,64,256]{3,2,1,0:T(8,128)}, f32[12,3,64,256]{3,2,1,0:T(8,128)}, f32[64,256]{1,0:T(8,128)}, f32[64,256]{1,0:T(8,128)}, ...), branch_computations={%region_0.0_spmd, %region_1.0_spmd, %region_2.0_spmd, %region_3.0_... | conditional | bytes 8 | solution.py:552
  3.9 55.4 %branch_1_fun.1 = (f32[72,3,64,256]{3,2,1,0:T(8,128)}, f32[8,8,128]{2,1,0:T(8,128)S(1)}) custom-call(s32[64]{0:T(128)S(1)} %get-tuple-element.66.plan, f32[12,3,64,256]{3,2,1,0:T(8,128)} %get-tuple-element.67.ens_hbm, f32[12,3,64,256]{3,2,1,0:T(8,128)} %get-tuple-element.68.pert_hbm, f32[64,256]{1,0:T(8,128)} %get-tuple-element.69.obs_hbm, ...), custom_call_target="tpu_custom_call" | custom-call | tf_op jit(solution)/shard_map/cond/branch_1_fun/pallas_call | solution.py:466
  59.8 3.7 %shard_map.78 = (f32[12]{0:T(128)}, f32[12,3,64,256]{3,2,1,0:T(8,128)}) custom-call(s32[64]{0:T(128)S(1)} %get-tuple-element.96.plan, f32[8,8,128]{2,1,0:T(8,128)S(1)} %get-tuple-element.98.lw_ref, f32[72,3,64,256]{3,2,1,0:T(8,128)} %get-tuple-element.99.slots), custom_call_target="tpu_custom_call" | custom-call | tf_op jit(solution)/shard_map/pallas_call | solution.py:525

commit v4 on v3

--- a/solution.py
+++ b/solution.py
@@ -16,8 +16,10 @@
 PART = 12
 CHIP = 24
 HALO = 6
-WIN = 18
-PER_TILE = 7
+STRIDE = 32
+GROUP = 4
+TILES = PART // GROUP
+PIECES = ((2, 6, 0), (0, 5, 6), (1, 5, 11), (3, 4, 16), (4, 2, 20), (6, 4, 22), (7, 4, 26))
 FAR = 6
 OPEN = 8
 CAPACITY = 24
@@ -154,28 +156,92 @@
     )(ancestors)
 
 
-def one_step(u, v, h, cor, obs, nud, force):
-    rows, lanes = u.shape
-    row = lax.broadcasted_iota(jnp.int32, u.shape, 0)
+def one_step(u_at, v_at, h_at, h_rows, v_rows, put_u, put_v, put_h, cor, obs, nud, force, tiles):
+    blocks = LAT // 8
+    lane = lax.broadcasted_iota(jnp.int32, (8, 128), 1)
+    lane_first, lane_last = lane == 0, lane == 127
 
     def across(q):
-        return pltpu.roll(q, lanes - 1, 1) - pltpu.roll(q, 1, 1)
-
-    def along(q):
-        above = jnp.where(row == rows - 1, 0.0, pltpu.roll(q, rows - 1, 0))
-        below = jnp.where(row == 0, 0.0, pltpu.roll(q, 1, 0))
-        return above - below
-
-    u_new = u + cor * v - 0.125 * across(h)
-    v_new = v - cor * u - 0.125 * along(h)
-    h_new = h - 0.125 * (across(u_new) + along(v_new)) + nud * (obs - h) + force
-    return u_new, v_new, h_new
+        after = [pltpu.roll(x, 127, 1) for x in q]
+        before = [pltpu.roll(x, 1, 1) for x in q]
+        if tiles == 1:
+            return [after[0] - before[0]]
+        return [
+            jnp.where(lane_last, after[1], after[0]) - before[0],
+            after[1] - jnp.where(lane_first, before[0], before[1]),
+        ]
+
+    def along(ref, r, t):
+        return ref[t, pl.ds(8 * r + 9, 8), :] - ref[t, pl.ds(8 * r + 7, 8), :]
+
+    dxu, centre = [], []
+
+    def finish(r):
+        for t in range(tiles):
+            x = centre[r][t]
+            put_h(
+                r, t,
+                x - 0.125 * (dxu[r][t] + along(v_rows, r, t)) + nud(r, t) * (obs(r, t) - x) + force(r, t),
+            )
+
+    for r in range(blocks):
+        h = [h_at(r, t) for t in range(tiles)]
+        centre.append(h)
+        dxh = across(h)
+        f = cor(r)
+        u_new = []
+        for t in range(tiles):
+            u, v = u_at(r, t), v_at(r, t)
+            u_new.append(u + f * v - 0.125 * dxh[t])
+            v_new = v - f * u - 0.125 * along(h_rows, r, t)
+            put_u(r, t, u_new[t])
+            put_v(r, t, v_new)
+            v_rows[t, 8 * r + 8:8 * r + 16, :] = v_new
+        dxu.append(across(u_new))
+        if r:
+            finish(r - 1)
+    finish(blocks - 1)
+
+
+def block(ref, lead, r, t):
+    return ref[(*lead, slice(8 * r, 8 * r + 8), slice(128 * t, 128 * t + 128))]
+
+
+def put(ref, lead, r, t, x):
+    ref[(*lead, slice(8 * r, 8 * r + 8), slice(128 * t, 128 * t + 128))] = x
+
+
+def three_steps(start, result, hs, vs, us, cor_v, obs, nud, force, tiles):
+    for r in range(LAT // 8):
+        for t in range(tiles):
+            hs[0, t, 8 * r + 8:8 * r + 16, :] = start(2, r, t)
+    for step in range(STEPS):
+        now, later, last = step % 2, (step + 1) % 2, step == STEPS - 1
+
+        def padded(ref, at):
+            return lambda r, t: ref[at, t, 8 * r + 8:8 * r + 16, :]
+
+        def store(f, ref):
+            def go(r, t, x):
+                if last:
+                    result(f, r, t, x)
+                elif f != 1:
+                    ref[later, t, 8 * r + 8:8 * r + 16, :] = x
+            return go
+
+        one_step(
+            (lambda r, t: start(0, r, t)) if step == 0 else padded(us, now),
+            (lambda r, t: start(1, r, t)) if step == 0 else padded(vs, now),
+            padded(hs, now), hs.at[now], vs.at[later],
+            store(0, us), store(1, vs), store(2, hs),
+            lambda r: block(cor_v, (), r, 0), obs, nud, functools.partial(force, step), tiles,
+        )
 
 
 def cycle_kernel(
     size, plan, ens_hbm, pert_hbm, obs_hbm, prec_hbm, nud_hbm,
     slots, lw_out,
-    ens, pert, fields, cor_v, pool, first, stage, msg_out, msg_in, win, edge,
+    ens, pert, fields, cor_v, pool, first, stage, msg_out, msg_in, edges, win, half, edge, hs, vs, us,
     misfit, zbuf, xbuf, lwbuf,
     in_sem, const_sem, halo_send, halo_recv, pool_send, pool_recv,
     edge_sem, ring_send, ring_recv, mir_send, mir_recv, out_sem,
@@ -221,6 +287,12 @@
     row_at = lax.broadcasted_iota(jnp.int32, (LAT, 128), 0).astype(F32)
     cor_v[...] = 0.3 * jnp.sin(math.pi * (row_at + 0.5 - LAT / 2) / LAT)
 
+    for ref in (hs, vs):
+        for n in range(2):
+            for t in range(2):
+                ref[n, t, 0:8, :] = jnp.zeros((8, 128), F32)
+                ref[n, t, LAT + 8:LAT + 16, :] = jnp.zeros((8, 128), F32)
+
     for cp in consts:
         cp.wait()
     for pair in loads:
@@ -241,20 +313,29 @@
         by = by % 128
         return x if by == 0 else pltpu.roll(x, by, 1)
 
-    def item(which, p):
-        i = which * PART + p if which < 5 else (60 if which == 6 else 61)
-        return i // 21, 6 * (i % 21)
-
-    items = [(f, p) for f in range(5) for p in range(PART)] + [(6, 0), (7, 0)]
+    within = lane & (STRIDE - 1)
+
+    def outer(which, p, q):
+        return turned(jnp.where(lane < 64, tile(which, p, 0), tile(which, p, 1)), STRIDE * q + HALO)
+
+    for which in range(8):
+        for group in range(TILES if which < 6 else 1):
+            start = acc = outer(which, group * GROUP, 0)
+            for q in range(1, GROUP):
+                acc = jnp.where(lane >= STRIDE * q - HALO, outer(which, group * GROUP + q, q), acc)
+            edges[which, group] = jnp.where(lane >= 128 - HALO, start, acc)
+
+    def spot(which, group):
+        return which, (group if which < 6 else 0)
+
     for side in range(2):
-        start = 0 if side == 0 else 122
-        acc = [None] * 3
-        for f, p in items:
-            t, o = item(f, p)
-            x = turned(tile(f, p, side), o - start)
-            acc[t] = x if acc[t] is None else jnp.where(lane >= o, x, acc[t])
-        for t in range(3):
-            msg_out[side, t] = acc[t]
+        for group in range(TILES):
+            acc = None
+            for which, width, to in PIECES:
+                source = HALO if side == 0 else HALO - width
+                x = turned(edges[spot(which, group)], to - source)
+                acc = x if acc is None else jnp.where(within >= to, x, acc)
+            msg_out[side, group] = acc
 
     pl.semaphore_wait(barrier, len(everyone))
     halos = [
@@ -268,12 +349,12 @@
         return remote(pool.at[at], pool.at[at], pool_send.at[p], pool_recv.at[p], sibling)
 
     def interior(p, carry):
-        cor = jnp.concatenate([cor_v[...], cor_v[...]], axis=1)
-        u, v, h = ens[p, 0], ens[p, 1], ens[p, 2]
-        for step in range(STEPS):
-            u, v, h = one_step(u, v, h, cor, fields[0], fields[2], pert[p, step])
         at = core * PART + p
-        pool[at, 0], pool[at, 1], pool[at, 2] = u, v, h
+        three_steps(
+            lambda f, r, t: block(ens, (p, f), r, t), lambda f, r, t, x: put(pool, (at, f), r, t, x),
+            hs, vs, us, cor_v, lambda r, t: block(fields, (0,), r, t), lambda r, t: block(fields, (2,), r, t),
+            lambda step, r, t: block(pert, (p, step), r, t), 2,
+        )
         share(at, p).start()
         return carry
 
@@ -282,38 +363,26 @@
     for s in range(2):
         remote(msg_out.at[s], msg_in.at[s], halo_send.at[s], halo_recv.at[s], sides[s]).wait_recv()
     for s in range(2):
-        for half in range(2):
-            members = list(range(half * PER_TILE, min(PART, (half + 1) * PER_TILE)))
-            for f in range(8):
-                if f >= 6 and half == 1:
-                    continue
-                count = PER_TILE if f >= 6 else len(members)
-                acc = None
-                for q in range(count):
-                    p = members[q] if f < 6 else 0
-                    o = WIN * q
-                    if s == 0:
-                        own, own_o = turned(tile(f, p, 0), o + HALO), o + HALO
-                        nb_o = o
-                    else:
-                        own, own_o = turned(tile(f, p, 1), o - 116), o
-                        nb_o = o + 2 * HALO
-                    parts = [(own_o, own)]
-                    if f != 5:
-                        t, io = item(f, p)
-                        nb = turned(msg_in[s, t], nb_o - io)
-                        parts.append((nb_o, nb))
-                    parts.sort(key=lambda e: e[0])
-                    for off, x in parts:
-                        acc = x if acc is None else jnp.where(lane >= off, x, acc)
-                win[s, half, f] = acc
-    for s in range(2):
-        for half in range(2):
-            u, v, h = win[s, half, 0], win[s, half, 1], win[s, half, 2]
-            for step in range(STEPS):
-                u, v, h = one_step(u, v, h, cor_v[...], win[s, 0, 6], win[s, 0, 7], win[s, half, 3 + step])
-            edge[core, s, half, 0], edge[core, s, half, 1], edge[core, s, half, 2] = u, v, h
-
+        for group in range(TILES):
+            for which, width, at in PIECES:
+                to = HALO - width if s == 0 else HALO
+                x = turned(msg_in[s, group], to - at)
+                inside = (within >= to) & (within < to + width)
+                win[s, which, group] = jnp.where(inside, x, edges[spot(which, group)])
+            win[s, 5, group] = edges[5, group]
+
+    def edge_group(n, carry):
+        for s in range(2):
+            three_steps(
+                lambda f, r, t: block(win, (s, f, n), r, t), lambda f, r, t, x: put(half, (s, f), r, t, x),
+                hs, vs, us, cor_v, lambda r, t: block(win, (s, 6, n), r, t),
+                lambda r, t: block(win, (s, 7, n), r, t), lambda step, r, t: block(win, (s, 3 + step, n), r, t), 1,
+            )
+        for f in range(3):
+            edge[core, n, f] = jnp.where((within >= HALO) & (within < 2 * HALO), half[0, f], half[1, f])
+        return carry
+
+    lax.fori_loop(0, TILES, edge_group, 0)
     edge_copy = remote(edge.at[core], edge.at[core], edge_sem.at[0], edge_sem.at[1], sibling)
     edge_copy.start()
     for p in range(PART):
@@ -323,14 +392,13 @@
     def whole(i):
         on = jnp.where(i >= PART, 1, 0)
         p = i - on * PART
-        half = jnp.where(p >= PER_TILE, 1, 0)
-        back = 128 - HALO - WIN * (p - half * PER_TILE)
+        group = lax.shift_right_logical(p, 2)
+        back = 128 - HALO - STRIDE * (p - GROUP * group)
         out = []
         for f in range(3):
-            left = pltpu.roll(edge[on, 0, half, f], back, 1)
-            right = pltpu.roll(edge[on, 1, half, f], back - HALO, 1)
-            low = jnp.where(lane < HALO, left, pool[i, f, :, 0:128])
-            high = jnp.where(lane >= 128 - HALO, right, pool[i, f, :, 128:256])
+            x = pltpu.roll(edge[on, group, f], back, 1)
+            low = jnp.where(lane < HALO, x, pool[i, f, :, 0:128])
+            high = jnp.where(lane >= 128 - HALO, x, pool[i, f, :, 128:256])
             out.append((low, high))
         return out
 
@@ -481,8 +549,13 @@
             pltpu.VMEM((2, most, 3, LAT, CLON), F32),
             pltpu.VMEM((2, 3, LAT, 128), F32),
             pltpu.VMEM((2, 3, LAT, 128), F32),
-            pltpu.VMEM((2, 2, 8, LAT, 128), F32),
-            pltpu.VMEM((2, 2, 2, 3, LAT, 128), F32),
+            pltpu.VMEM((8, TILES, LAT, 128), F32),
+            pltpu.VMEM((2, 8, TILES, LAT, 128), F32),
+            pltpu.VMEM((2, 3, LAT, 128), F32),
+            pltpu.VMEM((2, TILES, 3, LAT, 128), F32),
+            pltpu.VMEM((2, 2, LAT + 16, 128), F32),
+            pltpu.VMEM((2, 2, LAT + 16, 128), F32),
+            pltpu.VMEM((2, 2, LAT + 16, 128), F32),
             pltpu.VMEM((CHIP, 8, 128), F32),
             pltpu.VMEM((4, 8, 128), F32),
             pltpu.VMEM((4, 8, 128), F32),

time: 63.9 us -> 59.9 us (0.937)
  Pallas kernels: 61.5 us -> 58 us
    pallas_call x1, Pallas kernels: 55.4 us -> 52 us  [run_cycle(): pl.pallas_call(functools.partial(cycle_kernel, size), out_shape=(jax.Shap...]
where the time goes in v4:
time: 59.9 us; the launch traced here: 59.7 us
  Pallas kernels  58 us (97%)
  between operations  1.47 us (2%)
    pallas_call x1, Pallas kernels, run_cycle(): pl.pallas_call(functools.partial(cycle_kernel, size), out_shape=(jax.Shap...  52 us
    pallas_call x1, Pallas kernels, resample(): pl.pallas_call(resample_kernel, out_shape=(jax.ShapeDtypeStruct((PART,),...  3.68 us
    pallas_call x1, Pallas kernels, make_plan(): pl.pallas_call(plan_kernel, out_shape=(jax.ShapeDtypeStruct((64,), jnp.in...  2.38 us

profile of v4, /device:TPU:1, one launch (start us, length us, event | category | flops | bytes accessed | tf_op | source)
XLA Modules:
  0.0 59.7 jit_solution(10435670937294693925)
XLA Ops:
  0.6 2.4 %shard_map.77 = (s32[64]{0:T(128)S(1)}, s32[1]{0:T(128)}) custom-call(s32[96]{0:T(128)} %anc_ref.1), custom_call_target="tpu_custom_call" | custom-call | tf_op jit(solution)/shard_map/pallas_call | solution.py:146
  3.7 52.2 %conditional.1 = ((f32[72,3,64,256]{3,2,1,0:T(8,128)}, f32[8,8,128]{2,1,0:T(8,128)S(1)})) conditional(s32[]{:T(128)} %bitcast, (s32[64]{0:T(128)S(1)}, f32[12,3,64,256]{3,2,1,0:T(8,128)}, f32[12,3,64,256]{3,2,1,0:T(8,128)}, f32[64,256]{1,0:T(8,128)}, f32[64,256]{1,0:T(8,128)}, ...), branch_computations={%region_0.0_spmd, %region_1.0_spmd, %region_2.0_spmd, %region_3.0_... | conditional | bytes 8 | solution.py:625
  3.7 52.0 %branch_1_fun.1 = (f32[72,3,64,256]{3,2,1,0:T(8,128)}, f32[8,8,128]{2,1,0:T(8,128)S(1)}) custom-call(s32[64]{0:T(128)S(1)} %get-tuple-element.66.plan, f32[12,3,64,256]{3,2,1,0:T(8,128)} %get-tuple-element.67.ens_hbm, f32[12,3,64,256]{3,2,1,0:T(8,128)} %get-tuple-element.68.pert_hbm, f32[64,256]{1,0:T(8,128)} %get-tuple-element.69.obs_hbm, ...), custom_call_target="tpu_custom_call" | custom-call | tf_op jit(solution)/shard_map/cond/branch_1_fun/pallas_call | solution.py:534
  55.9 3.7 %shard_map.78 = (f32[12]{0:T(128)}, f32[12,3,64,256]{3,2,1,0:T(8,128)}) custom-call(s32[64]{0:T(128)S(1)} %get-tuple-element.96.plan, f32[8,8,128]{2,1,0:T(8,128)S(1)} %get-tuple-element.98.lw_ref, f32[72,3,64,256]{3,2,1,0:T(8,128)} %get-tuple-element.99.slots), custom_call_target="tpu_custom_call" | custom-call | tf_op jit(solution)/shard_map/pallas_call | solution.py:598

commit v5 on v4

--- a/solution.py
+++ b/solution.py
@@ -20,10 +20,10 @@
 GROUP = 4
 TILES = PART // GROUP
 PIECES = ((2, 6, 0), (0, 5, 6), (1, 5, 11), (3, 4, 16), (4, 2, 20), (6, 4, 22), (7, 4, 26))
-FAR = 6
-OPEN = 8
 CAPACITY = 24
-LEVELS = (12, 13, 14, 16, 24)
+WIDE = (CAPACITY, 6, 8)
+NARROW = (4, 6)
+LEVELS = tuple((size, *NARROW) for size in (11, 12, 13, 14, 16)) + (WIDE,)
 SLOTS = CHIP + 2 * CAPACITY
 GATHER_AT = 2 * CAPACITY
 
@@ -54,17 +54,10 @@
     c2 = [counts[d, 2] for d in range(4)]
     c3 = [counts[d, 3] for d in range(4)]
 
+    limit, free = NARROW
+
     def clamp(d, x):
-        return jnp.minimum(jnp.maximum(x, jnp.maximum(0, c2[d] - FAR)), jnp.minimum(FAR, c2[d]))
-
-    def worst(a):
-        top = jnp.int32(0)
-        for s in range(4):
-            d1, d2, u1 = (s - 1) % 4, (s - 2) % 4, (s + 1) % 4
-            down = jnp.maximum(OPEN, a[d2] + c1[d1]) + a[d1]
-            up = jnp.maximum(OPEN, c2[d2] - a[d2] + c3[u1]) + c2[u1] - a[u1]
-            top = jnp.maximum(top, jnp.maximum(down, up))
-        return top
+        return jnp.minimum(jnp.maximum(x, jnp.maximum(0, c2[d] - limit)), jnp.minimum(limit, c2[d]))
 
     a = [clamp(d, lax.shift_right_arithmetic(c2[d] + c3[d] - c1[d] + 1, 1)) for d in range(4)]
     for d in range(4):
@@ -79,11 +72,20 @@
         m = jnp.maximum(down((d + 2) % 4), down((d + 1) % 4)) - a[d]
         n = jnp.maximum(up((d + 2) % 4), up((d + 3) % 4)) - b[d]
         a[d] = clamp(d, lax.shift_right_arithmetic(n + c2[d] - m + 1, 1))
-    top = worst(a)
-    half = [lax.shift_right_logical(c2[d] + 1, 1) for d in range(4)]
-    fits = top <= CAPACITY
-    a = [jnp.where(fits, a[d], half[d]) for d in range(4)]
-    top = jnp.where(fits, top, CAPACITY)
+    top = jnp.int32(0)
+    for s in range(4):
+        d1, d2, u1 = (s - 1) % 4, (s - 2) % 4, (s + 1) % 4
+        below = jnp.maximum(free, a[d2] + c1[d1]) + a[d1]
+        above = jnp.maximum(free, c2[d2] - a[d2] + c3[u1]) + c2[u1] - a[u1]
+        top = jnp.maximum(top, jnp.maximum(below, above))
+        top = jnp.where(c2[s] > 2 * limit, CAPACITY, top)
+    narrow = top <= LEVELS[-2][0]
+    a = [jnp.where(narrow, a[d], lax.shift_right_logical(c2[d] + 1, 1)) for d in range(4)]
+    opened = jnp.where(narrow, free, WIDE[2])
+    level = jnp.int32(0)
+    for size, _, _ in LEVELS[:-1]:
+        level = level + jnp.where(top > size, 1, 0)
+    level_ref[0] = level
     b = [c2[d] - a[d] for d in range(4)]
 
     def at(values, index):
@@ -100,26 +102,26 @@
     d1, d2, u1 = lax.rem(chip + 3, 4), lax.rem(chip + 2, 4), lax.rem(chip + 1, 4)
     far_row = (d2 * 4 + 2) * 32
     a_far, b_far = at(a, d2), at(b, d2)
-    down_fwd = jnp.maximum(OPEN, a_far + at(c1, d1))
-    up_fwd = jnp.maximum(OPEN, b_far + at(c3, u1))
+    down_fwd = jnp.maximum(opened, a_far + at(c1, d1))
+    up_fwd = jnp.maximum(opened, b_far + at(c3, u1))
     for i in range(CAPACITY):
         plan_ref[i] = 0
         plan_ref[CAPACITY + i] = 0
-    for i in range(FAR):
+    for i in range(WIDE[1]):
         plan_ref[i] = entry(far_row, i)
         plan_ref[CAPACITY + i] = entry(far_row, a_far + i)
     for i in range(PART):
         plan_ref[a_far + i] = entry((d1 * 4 + 1) * 32, i)
         plan_ref[CAPACITY + b_far + i] = entry((u1 * 4 + 3) * 32, i)
-    for i in range(FAR):
+    for i in range(WIDE[1]):
         plan_ref[down_fwd + i] = CHIP + i
         plan_ref[CAPACITY + up_fwd + i] = CHIP + i
 
     own_a = at(a, chip)
     from_up = at(a, chip + 3)
     from_down = at(b, chip + 1)
-    far_down = jnp.maximum(OPEN, at(a, chip + 3) + at(c1, chip))
-    far_up = jnp.maximum(OPEN, at(b, chip + 1) + at(c3, chip))
+    far_down = jnp.maximum(opened, at(a, chip + 3) + at(c1, chip))
+    far_up = jnp.maximum(opened, at(b, chip + 1) + at(c3, chip))
     for j in range(PART):
         old = anc_ref[member * PART + j]
         src = third(old)
@@ -136,10 +138,6 @@
             ),
         )
         plan_ref[GATHER_AT + j] = where
-    level = jnp.int32(0)
-    for size in LEVELS[:-1]:
-        level = level + jnp.where(top > size, 1, 0)
-    level_ref[0] = level
 
 
 def make_plan(ancestors):
@@ -239,7 +237,7 @@
 
 
 def cycle_kernel(
-    size, plan, ens_hbm, pert_hbm, obs_hbm, prec_hbm, nud_hbm,
+    level, plan, ens_hbm, pert_hbm, obs_hbm, prec_hbm, nud_hbm,
     slots, lw_out,
     ens, pert, fields, cor_v, pool, first, stage, msg_out, msg_in, edges, win, half, edge, hs, vs, us,
     misfit, zbuf, xbuf, lwbuf,
@@ -247,6 +245,7 @@
     edge_sem, ring_send, ring_recv, mir_send, mir_recv, out_sem,
     z_send, z_recv, x_send, x_recv, m_send, m_recv,
 ):
+    size, far, opened = level
     member, lon = lax.axis_index("member"), lax.axis_index("lon")
     core = lax.rem(member, 2)
     lon_x, lon_z = lax.div(lon, 4), lax.rem(lon, 4)
@@ -295,9 +294,6 @@
 
     for cp in consts:
         cp.wait()
-    for pair in loads:
-        for cp in pair:
-            cp.wait()
 
     lane = lax.broadcasted_iota(jnp.int32, (LAT, 128), 1)
 
@@ -318,18 +314,19 @@
     def outer(which, p, q):
         return turned(jnp.where(lane < 64, tile(which, p, 0), tile(which, p, 1)), STRIDE * q + HALO)
 
-    for which in range(8):
-        for group in range(TILES if which < 6 else 1):
+    def spot(which, group):
+        return which, (group if which < 6 else 0)
+
+    for group in range(TILES):
+        for cp in loads[group]:
+            cp.wait()
+        for which in range(8 if group == 0 else 6):
             start = acc = outer(which, group * GROUP, 0)
             for q in range(1, GROUP):
                 acc = jnp.where(lane >= STRIDE * q - HALO, outer(which, group * GROUP + q, q), acc)
             edges[which, group] = jnp.where(lane >= 128 - HALO, start, acc)
 
-    def spot(which, group):
-        return which, (group if which < 6 else 0)
-
-    for side in range(2):
-        for group in range(TILES):
+        for side in range(2):
             acc = None
             for which, width, to in PIECES:
                 source = HALO if side == 0 else HALO - width
@@ -345,8 +342,9 @@
     for cp in halos:
         cp.start()
 
-    def share(at, p):
-        return remote(pool.at[at], pool.at[at], pool_send.at[p], pool_recv.at[p], sibling)
+    def share(on_core, group):
+        part = pool.at[pl.ds(on_core * PART + GROUP * group, GROUP)]
+        return remote(part, part, pool_send.at[group], pool_recv.at[group], sibling)
 
     def interior(p, carry):
         at = core * PART + p
@@ -355,24 +353,30 @@
             hs, vs, us, cor_v, lambda r, t: block(fields, (0,), r, t), lambda r, t: block(fields, (2,), r, t),
             lambda step, r, t: block(pert, (p, step), r, t), 2,
         )
-        share(at, p).start()
         return carry
 
-    lax.fori_loop(0, PART, interior, 0)
+    def interiors(group, carry):
+        lax.fori_loop(GROUP * group, GROUP * group + GROUP, interior, 0)
+        share(core, group).start()
+        return carry
+
+    lax.fori_loop(0, TILES, interiors, 0)
 
     for s in range(2):
         remote(msg_out.at[s], msg_in.at[s], halo_send.at[s], halo_recv.at[s], sides[s]).wait_recv()
-    for s in range(2):
-        for group in range(TILES):
+
+    def edge_copy(on_core, group):
+        part = edge.at[on_core, group]
+        return remote(part, part, edge_sem.at[0, group], edge_sem.at[1, group], sibling)
+
+    def edge_group(n, carry):
+        for s in range(2):
             for which, width, at in PIECES:
                 to = HALO - width if s == 0 else HALO
-                x = turned(msg_in[s, group], to - at)
+                x = turned(msg_in[s, n], to - at)
                 inside = (within >= to) & (within < to + width)
-                win[s, which, group] = jnp.where(inside, x, edges[spot(which, group)])
-            win[s, 5, group] = edges[5, group]
-
-    def edge_group(n, carry):
-        for s in range(2):
+                win[s, which, n] = jnp.where(inside, x, edges[which, n if which < 6 else 0])
+            win[s, 5, n] = edges[5, n]
             three_steps(
                 lambda f, r, t: block(win, (s, f, n), r, t), lambda f, r, t, x: put(half, (s, f), r, t, x),
                 hs, vs, us, cor_v, lambda r, t: block(win, (s, 6, n), r, t),
@@ -380,14 +384,14 @@
             )
         for f in range(3):
             edge[core, n, f] = jnp.where((within >= HALO) & (within < 2 * HALO), half[0, f], half[1, f])
+        edge_copy(core, n).start()
         return carry
 
     lax.fori_loop(0, TILES, edge_group, 0)
-    edge_copy = remote(edge.at[core], edge.at[core], edge_sem.at[0], edge_sem.at[1], sibling)
-    edge_copy.start()
-    for p in range(PART):
-        share((1 - core) * PART + p, p).wait_recv()
-    remote(edge.at[1 - core], edge.at[1 - core], edge_sem.at[0], edge_sem.at[1], sibling).wait_recv()
+    for group in range(TILES):
+        share(1 - core, group).wait_recv()
+    for group in range(TILES):
+        edge_copy(1 - core, group).wait_recv()
 
     def whole(i):
         on = jnp.where(i >= PART, 1, 0)
@@ -403,7 +407,7 @@
         return out
 
     positions = (size + 1) // 2
-    open_pos, far_pos = OPEN // 2, FAR // 2
+    open_pos, far_pos = opened // 2, far // 2
 
     def split(pos):
         return 2 * pos + 1 == size
@@ -437,8 +441,8 @@
                 stage[way, pos, f, :, 0:128], stage[way, pos, f, :, 128:256] = parts[f]
             ring_copy(way, pos).start()
 
-    for p in range(PART):
-        share(core * PART + p, p).wait_send()
+    for group in range(TILES):
+        share(core, group).wait_send()
 
     def complete(i, carry):
         parts = whole(i)
@@ -493,7 +497,7 @@
             mirror_copy(way, pos, 1 - core).wait_recv()
     for way in range(2):
         cp = pltpu.make_async_copy(
-            first.at[way], slots.at[pl.ds(CHIP + way * CAPACITY, FAR)], out_sem.at[1 + way]
+            first.at[way], slots.at[pl.ds(CHIP + way * CAPACITY, far)], out_sem.at[1 + way]
         )
         cp.start()
         keep.append(cp)
@@ -501,7 +505,7 @@
         for way in range(2):
             idx = plan[way * CAPACITY + entry_at(pos, core)]
             own = pool[jnp.minimum(idx, CHIP - 1)]
-            passed = first[way, jnp.clip(idx - CHIP, 0, FAR - 1)]
+            passed = first[way, jnp.clip(idx - CHIP, 0, far - 1)]
             stage[way, pos] = jnp.where(idx < CHIP, own, passed)
             ring_copy(way, pos).start()
     for pos in range(far_pos, positions):
@@ -513,8 +517,10 @@
         cp.wait_send()
         cp.wait_recv()
     lw_out[...] = lwbuf[...]
-    for cp in halos + [edge_copy]:
+    for cp in halos:
         cp.wait_send()
+    for group in range(TILES):
+        edge_copy(core, group).wait_send()
     for pos in range(positions):
         for way in range(2):
             ring_copy(way, pos).wait_send()
@@ -527,12 +533,12 @@
         cp.wait()
 
 
-def run_cycle(size, number, plan, ensemble, perturbation, observed, precision, nudging):
+def run_cycle(level, number, plan, ensemble, perturbation, observed, precision, nudging):
     anywhere = pl.BlockSpec(memory_space=pltpu.HBM)
     dma = pltpu.SemaphoreType.DMA
-    most = (size + 1) // 2
+    most = (level[0] + 1) // 2
     return pl.pallas_call(
-        functools.partial(cycle_kernel, size),
+        functools.partial(cycle_kernel, level),
         out_shape=(
             jax.ShapeDtypeStruct((SLOTS, 3, LAT, CLON), F32),
             jax.ShapeDtypeStruct((8, 8, 128), F32),
@@ -545,7 +551,7 @@
             pltpu.VMEM((3, LAT, CLON), F32),
             pltpu.VMEM((LAT, 128), F32),
             pltpu.VMEM((CHIP, 3, LAT, CLON), F32),
-            pltpu.VMEM((2, FAR, 3, LAT, CLON), F32),
+            pltpu.VMEM((2, level[1], 3, LAT, CLON), F32),
             pltpu.VMEM((2, most, 3, LAT, CLON), F32),
             pltpu.VMEM((2, 3, LAT, 128), F32),
             pltpu.VMEM((2, 3, LAT, 128), F32),
@@ -560,7 +566,7 @@
             pltpu.VMEM((4, 8, 128), F32),
             pltpu.VMEM((4, 8, 128), F32),
             pltpu.VMEM((8, 8, 128), F32),
-            dma((2, 3)), dma((3,)), dma((2,)), dma((2,)), dma((PART,)), dma((PART,)), dma((2,)),
+            dma((2, 3)), dma((3,)), dma((2,)), dma((2,)), dma((TILES,)), dma((TILES,)), dma((2, TILES)),
             dma((2, most)), dma((2, most)), dma((2, most)), dma((2, most)), dma((3,)),
             dma((3,)), dma((3,)), dma((3,)), dma((3,)), dma((7,)), dma((7,)),
         ],
@@ -618,7 +624,7 @@
 def body(ensemble, perturbation, observed, precision, nudging, ancestors):
     plan, level = make_plan(ancestors)
     operands = (plan, ensemble, perturbation, observed, precision, nudging)
-    branches = [functools.partial(run_cycle, size, n) for n, size in enumerate(LEVELS)]
+    branches = [functools.partial(run_cycle, form, n) for n, form in enumerate(LEVELS)]
     if len(branches) == 1:
         slots, lw = branches[0](*operands)
     else:

time: 59.9 us -> 56.6 us (0.945); the launches traced: 59.7 us -> 55.4 us
  Pallas kernels: 58 us -> 53.7 us
    pallas_call x1, Pallas kernels: 52 us -> 47.3 us  [run_cycle(): pl.pallas_call(functools.partial(cycle_kernel, level), out_shape=(jax.Sha...]
where the time goes in v5:
time: 56.6 us; the launch traced here: 55.4 us
  Pallas kernels  53.7 us (95%)
  between operations  1.47 us (3%)
    pallas_call x1, Pallas kernels, run_cycle(): pl.pallas_call(functools.partial(cycle_kernel, level), out_shape=(jax.Sha...  47.3 us
    pallas_call x1, Pallas kernels, resample(): pl.pallas_call(resample_kernel, out_shape=(jax.ShapeDtypeStruct((PART,),...  4.05 us
    pallas_call x1, Pallas kernels, make_plan(): pl.pallas_call(plan_kernel, out_shape=(jax.ShapeDtypeStruct((64,), jnp.in...  2.38 us

profile of v5, /device:TPU:1, one launch (start us, length us, event | category | flops | bytes accessed | tf_op | source)
XLA Modules:
  0.0 55.4 jit_solution(15841042937877618969)
XLA Ops:
  0.6 2.4 %shard_map.77 = (s32[64]{0:T(128)S(1)}, s32[1]{0:T(128)}) custom-call(s32[96]{0:T(128)} %anc_ref.1), custom_call_target="tpu_custom_call" | custom-call | tf_op jit(solution)/shard_map/pallas_call | solution.py:144
  3.7 47.5 %conditional.1 = ((f32[72,3,64,256]{3,2,1,0:T(8,128)}, f32[8,8,128]{2,1,0:T(8,128)S(1)})) conditional(s32[]{:T(128)} %bitcast, (s32[64]{0:T(128)S(1)}, f32[12,3,64,256]{3,2,1,0:T(8,128)}, f32[12,3,64,256]{3,2,1,0:T(8,128)}, f32[64,256]{1,0:T(8,128)}, f32[64,256]{1,0:T(8,128)}, ...), branch_computations={%region_0.0_spmd, %region_1.0_spmd, %region_2.0_spmd, %region_3.0_... | conditional | bytes 8 | solution.py:631
  3.7 47.3 %branch_0_fun.1 = (f32[72,3,64,256]{3,2,1,0:T(8,128)}, f32[8,8,128]{2,1,0:T(8,128)S(1)}) custom-call(s32[64]{0:T(128)S(1)} %get-tuple-element.72.plan, f32[12,3,64,256]{3,2,1,0:T(8,128)} %get-tuple-element.73.ens_hbm, f32[12,3,64,256]{3,2,1,0:T(8,128)} %get-tuple-element.74.pert_hbm, f32[64,256]{1,0:T(8,128)} %get-tuple-element.75.obs_hbm, ...), custom_call_target="tpu_custom_call" | custom-call | tf_op jit(solution)/shard_map/cond/branch_0_fun/pallas_call | solution.py:540
  51.2 4.1 %shard_map.78 = (f32[12]{0:T(128)}, f32[12,3,64,256]{3,2,1,0:T(8,128)}) custom-call(s32[64]{0:T(128)S(1)} %get-tuple-element.114.plan, f32[8,8,128]{2,1,0:T(8,128)S(1)} %get-tuple-element.116.lw_ref, f32[72,3,64,256]{3,2,1,0:T(8,128)} %get-tuple-element.117.slots), custom_call_target="tpu_custom_call" | custom-call | tf_op jit(solution)/shard_map/pallas_call | solution.py:604
